TPU v7x, 128 devices: a whole 4x4x4 slice. The times are simulated.
128 devices in a mesh: dev: 128 (over z, y, x, core).
Axes of the slice: x: 4, y: 4, z: 4, core: 2. Of those that a mesh axis runs over, the one named last changes fastest.
Arguments:
- logits: float32 [32768, 32], P('dev'), may hold values from -8 to 404
- route_cost: float32 [32768, 32], P('dev'), may hold values from 0.1 to 4
- capacity: int32 [8192, 128], P('dev'), may hold values from 0 to 3
- send_route: int32 [128, 128, 64], P('dev'), may hold values from -1 to 8191, as said below
- recv_piece: int32 [4, 128, 128, 64], P(None, 'dev'), may hold values from 0 to 8191, as said below
Outputs:
- demand: float32 [8192, 128], P('dev')
- grad_logits: float32 [32768, 32], P('dev')
Inputs may be any that keep to these rules, and one draw needn't show every extreme that they name: `send_route`: the live slots of each block to one owner come first; -1 marks the rest. At most 64 pieces go from one device to one owner; in every draw a few owners, drawn anew, receive exactly 64 from every device. `recv_piece`: slot j of source s's block at owner d describes the piece of send_route's entry (s, d, j): the same route index; first cell plus number of cells is at most 128; empty slots hold four zeros.
All inputs are finite; a program needn't handle non-finite values.
Results may differ from a plain program's by a relative error of at most 0.000037.
Values sent between devices are 32-bit elements; how exact they have to be, the bound alone decides.
No kernel may reach another device: no remote copies, remote signals or barrier semaphores. Data moves between devices by JAX's collectives and lax.ppermute only.
A program may use at most 64 MiB of HBM per device.

v0:
```python
import jax
import jax.numpy as jnp
from jax import lax
from jax.sharding import PartitionSpec as P

SHARPNESS = 2.0


def body(logits, route_cost, capacity, send_route, recv_piece):
    net_count, cand_count = logits.shape
    probabilities = jax.nn.softmax(logits, axis=-1)
    flat_probs = probabilities.reshape(-1)
    route_total = net_count * cand_count
    row_count, cell_count = capacity.shape
    total_cells = row_count * cell_count
    route_in = recv_piece[0, 0]
    tile_in = recv_piece[1, 0]
    piece_lo = recv_piece[2, 0]
    piece_len = recv_piece[3, 0]
    targets = send_route[0]
    source_count, slot_count = targets.shape
    is_live = piece_len > 0
    everything = lax.all_gather(flat_probs, "dev", axis=0, tiled=True)
    source_ids = lax.broadcasted_iota(jnp.int32, (source_count, slot_count), 0)
    weight = everything[source_ids * route_total + route_in]
    weight = jnp.where(is_live, weight, 0.0)
    piece_start = tile_in * cell_count + piece_lo
    piece_stop = jnp.where(piece_lo + piece_len < cell_count, piece_start + piece_len, total_cells)
    diff_marks = jnp.zeros((total_cells,), jnp.float32)
    diff_marks = diff_marks.at[piece_start.reshape(-1)].add(weight.reshape(-1))
    diff_marks = diff_marks.at[piece_stop.reshape(-1)].add(-weight.reshape(-1), mode="drop")
    demand = jnp.cumsum(diff_marks.reshape(row_count, cell_count), axis=1)
    pressure = jax.nn.sigmoid(SHARPNESS * (demand - capacity.astype(jnp.float32)))
    prefix = jnp.cumsum(pressure, axis=1).reshape(-1)
    upper_sum = prefix[jnp.clip(piece_start + piece_len - 1, 0, total_cells - 1)]
    lower_sum = jnp.where(piece_lo > 0, prefix[jnp.clip(piece_start - 1, 0, total_cells - 1)], 0.0)
    slot_grad = jnp.where(is_live, upper_sum - lower_sum, 0.0)
    returned = lax.all_to_all(slot_grad, "dev", split_axis=0, concat_axis=0, tiled=True)
    target_index = jnp.where(targets >= 0, targets, route_total)
    route_grad = (
        route_cost.reshape(-1).at[target_index.reshape(-1)].add(returned.reshape(-1), mode="drop")
    )
    route_grad = route_grad.reshape(net_count, cand_count)
    expected = jnp.sum(probabilities * route_grad, axis=-1, keepdims=True)
    return (demand, probabilities * (route_grad - expected))


def solution(mesh):
    placed = (
        P("dev", None),
        P("dev", None),
        P("dev", None),
        P("dev", None, None),
        P(None, "dev", None, None),
    )
    return jax.shard_map(
        body,
        mesh=mesh,
        in_specs=placed,
        out_specs=(P("dev", None), P("dev", None)),
        check_vma=False,
    )
```

profile of v0, /device:TPU:1, one launch (start us, length us, event | category | flops | bytes accessed | tf_op | source)
XLA Modules:
  0.0 565.3 jit_solution(6523480253693915859)
XLA Ops:
  7.2 0.9 copy.18
  8.1 0.8 reduce_max.9
  8.8 0.2 fusion.1
  9.0 0.1 fusion
  9.2 0.7 reshape.309
  9.9 0.8 fusion.5
  12.0 0.9 copy.21
  13.1 69.2 %all-gather.2.cloned.1.call-done = f32[1048576]{0:T(1024)} async-done(((f32[8192]{0:T(1024)}), f32[1048576]{0:T(1024)}) %all-gather.2.cloned.1.call-update) | async-done | bytes 4194320 | tf_op jit(solution)/shard_map/all_gather | solution.py:23
  82.2 215.1 %gather_fusion = f32[8192]{0:T(1024)S(1)} fusion(f32[1048576]{0:T(1024)} %all-gather.2.cloned.1.call-done, s32[8192]{0:T(1024)S(1)} %broadcast_clamp_fusion.2), kind=kCustom, calls=%fused_computation | custom fusion | bytes 98304 | tf_op jit(solution)/shard_map/gather | solution.py:25
  297.4 51.1 %scatter_custom_fusion = f32[8192]{0:T(1024)S(1)} fusion(s32[8192]{0:T(1024)S(1)} %bitcast.37, f32[8192]{0:T(1024)S(1)} %get-tuple-element.7, f32[]{:T(128)} %constant.10.clone.1), kind=kCustom, calls=%fused_computation.27 | custom fusion | flops 8192 | bytes 32772 | tf_op jit(solution)/shard_map/scatter-add | solution.py:30
  348.5 51.9 %scatter_fusion = f32[8192]{0:T(1024)S(1)} fusion(f32[8192]{0:T(1024)S(1)} %scatter_custom_fusion, s32[8192]{0:T(1024)S(1)} %bitcast.35, f32[8192]{0:T(1024)S(1)} %get-tuple-element.6), kind=kCustom, calls=%fused_computation.4 | custom fusion | flops 8192 | bytes 131072 | tf_op jit(solution)/shard_map/scatter-add | solution.py:31
  400.3 0.3 reduce_window_sum.17
  400.7 0.3 reduce_window_sum.18
  401.0 45.5 %gather_fusion.2 = f32[8192]{0:T(1024)S(1)} fusion(f32[8192]{0:T(1024)S(1)} %bitcast.32, s32[8192]{0:T(1024)S(1)} %broadcast_clamp_fusion), kind=kCustom, calls=%fused_computation.2 | custom fusion | bytes 98304 | tf_op jit(solution)/shard_map/gather | solution.py:36
  446.6 45.5 %gather_fusion.1 = f32[8192]{0:T(1024)S(1)} fusion(f32[8192]{0:T(1024)S(1)} %bitcast.33, s32[8192]{0:T(1024)S(1)} %broadcast_clamp_fusion.1), kind=kCustom, calls=%fused_computation.1 | custom fusion | bytes 98304 | tf_op jit(solution)/shard_map/gather | solution.py:35
  492.2 0.6 subtract_select_fusion
  492.8 9.1 %all-to-all-start = ((f32[128,1,64]{2,1,0:T(1,128)}), f32[128,1,64]{2,1,0:T(1,128)S(1)}, u32[]{:S(2)}, u32[]{:S(2)}) async-start(f32[128,1,64]{2,1,0:T(1,128)} %bitcast.10), calls=%async_computation | async-start | bytes 131072 | tf_op jit(solution)/shard_map/all_to_all | solution.py:38
  502.2 9.3 %all-to-all-done = f32[128,1,64]{2,1,0:T(1,128)S(1)} async-done(((f32[128,1,64]{2,1,0:T(1,128)}), f32[128,1,64]{2,1,0:T(1,128)S(1)}, u32[]{:S(2)}, u32[]{:S(2)}) %all-to-all-start) | async-done | bytes 32800 | tf_op jit(solution)/shard_map/all_to_all | solution.py:38
  511.6 0.5 broadcast.342
  512.1 0.8 reduce.3
  513.0 44.2 %scatter_fusion.1 = f32[8192]{0:T(1024)S(1)} fusion(f32[8192]{0:T(1024)S(1)} %reshape.311, s32[8192]{0:T(1024)S(1)} %bitcast.36, f32[8192]{0:T(1024)S(1)} %reshape.362), kind=kCustom, calls=%fused_computation.5 | custom fusion | flops 8192 | bytes 131072 | tf_op jit(solution)/shard_map/scatter-add | solution.py:41
  557.3 0.2 multiply_reduce_fusion
  557.5 0.2 subtract_multiply_fusion
  557.7 0.7 copy.23
  (38 shorter events, 2.0 us)
Async XLA Ops:
  7.2 75.1 %all-gather.2.cloned.1.call-start = ((), (), s32[]{:S(2)}) async-start(), calls=%async_computation.1 | async-start | bytes 4227072 | tf_op jit(solution)/shard_map/all_gather | solution.py:23
  348.4 52.2 %copy-start.1 = (s32[64,128]{1,0:T(8,128)S(1)}, s32[64,128]{1,0:T(8,128)}, u32[]{:S(2)}) copy-start(s32[64,128]{1,0:T(8,128)} %param.7) | copy-start | bytes 98308
  400.6 45.9 %copy-start = (f32[64,128]{1,0:T(8,128)}, f32[64,128]{1,0:T(8,128)S(1)}, u32[]{:S(2)}) copy-start(f32[64,128]{1,0:T(8,128)S(1)} %reduce_window_sum.17) | copy-start | bytes 98308
  446.6 55.4 %copy-start.2 = (f32[256,32]{0,1:T(8,128)S(1)}, f32[256,32]{0,1:T(8,128)}, u32[]{:S(2)}) copy-start(f32[256,32]{0,1:T(8,128)} %param.6) | copy-start | bytes 98308
  492.8 18.7 %all-to-all-start = ((f32[128,1,64]{2,1,0:T(1,128)}), f32[128,1,64]{2,1,0:T(1,128)S(1)}, u32[]{:S(2)}, u32[]{:S(2)}) async-start(f32[128,1,64]{2,1,0:T(1,128)} %bitcast.10), calls=%async_computation | async-start | bytes 131072 | tf_op jit(solution)/shard_map/all_to_all | solution.py:38
Sparse Core Ops, SparseCore 0:
  11.7 70.4 all-gather.1
where the time goes:
time: 572 us; the launch traced here: 565 us
  local copies, waits for them, and re-layouts  312 us (55%)
  other arithmetic  151 us (26%)
  waiting for transfers between devices  78.5 us (14%)
  between operations  14.3 us (2%)
  starting transfers between devices  9.16 us (2%)
    gather x1, local copies, waits for them, and re-layouts, body(): weight = everything[source_ids * route_total + route_in]  215 us
    all_gather x1, waiting for transfers between devices, body(): everything = lax.all_gather(flat_probs, 'dev', axis=0, tiled=True)  69.2 us
    scatter-add x1, other arithmetic, body(): diff_marks.at[piece_stop.reshape(-1)].add(-weight.reshape(-1), mode='drop')  51.9 us
    scatter-add x1, other arithmetic, body(): diff_marks = diff_marks.at[piece_start.reshape(-1)].add(weight.reshape(-1))  51.1 us
    gather x2, local copies, waits for them, and re-layouts, body(): prefix[jnp.clip(piece_start - 1, 0, total_cells - 1)]  45.6 us
    gather x2, local copies, waits for them, and re-layouts, body(): prefix[jnp.clip(piece_start + piece_len - 1, 0, total_cells - 1)]  45.6 us
    scatter-add x1, other arithmetic, body(): route_cost.reshape(-1).at[target_index.reshape(-1)]  44.2 us
  transfers between devices with their start and end apart: 2, of which 2 were waited for; matrix products, arithmetic and copies ran while one was open for 1% of the time, Pallas kernels for 0%

commit v1 on v0

v1 whole, which is shorter than its diff:
```python
import jax
import jax.numpy as jnp
from jax import lax
from jax.experimental import pallas as pl
from jax.experimental.pallas import tpu as pltpu
from jax.sharding import PartitionSpec as P

SHARPNESS = 2.0
BF = jnp.bfloat16
F32 = jnp.float32
ROWS = 8


def split3(x):
    hi = x.astype(BF)
    rest = x - hi.astype(F32)
    mid = rest.astype(BF)
    low = (rest - mid.astype(F32)).astype(BF)
    return hi, mid, low


def iota_bf(shape):
    return lax.broadcasted_iota(jnp.int32, shape, 0).astype(F32).astype(BF)


def to_bf(x):
    return x.astype(F32).astype(BF)


def one_hot(ids_row, iota):
    ids = jnp.broadcast_to(ids_row, iota.shape)
    return jnp.where(iota == ids, jnp.ones(iota.shape, BF), jnp.zeros(iota.shape, BF))


def gather_kernel(logits_ref, send_ref, weight_ref, prob_ref, held_ref):
    cands, nets = logits_ref.shape
    slots, owners = send_ref.shape
    scores = logits_ref[...]
    powers = jnp.exp(scores - jnp.max(scores, axis=0, keepdims=True))
    probs = powers / jnp.sum(powers, axis=0, keepdims=True)
    prob_ref[...] = probs
    table = jnp.concatenate(split3(probs), axis=0)
    net_iota = iota_bf((nets, owners))
    cand_iota = lax.broadcasted_iota(jnp.int32, (cands, owners), 0)

    def step(i, carry):
        base = pl.multiple_of(i * ROWS, ROWS)
        routes = send_ref[pl.ds(base, ROWS), :]
        net_ids = to_bf(lax.shift_right_arithmetic(routes, 5))
        cand_ids = lax.bitwise_and(routes, 31)
        rows = []
        for j in range(0, ROWS, 2):
            spread = jnp.concatenate(
                [one_hot(net_ids[j + h : j + h + 1], net_iota) for h in range(2)], axis=1
            )
            found = jnp.dot(table, spread, preferred_element_type=F32)
            found = found[:cands] + found[cands : 2 * cands] + found[2 * cands :]
            for h in range(2):
                part = found[:, h * owners : (h + 1) * owners]
                keep = cand_iota == cand_ids[j + h : j + h + 1]
                rows.append(jnp.sum(jnp.where(keep, part, 0.0), axis=0, keepdims=True))
        held_ref[pl.ds(base, ROWS), :] = jnp.concatenate(rows, axis=0)
        return carry

    lax.fori_loop(0, slots // ROWS, step, 0)
    weight_ref[...] = held_ref[...].T


def cells_kernel(weight_ref, piece_ref, capacity_ref, demand_ref, grad_ref, held_ref, total_ref, back_ref):
    slots, sources = held_ref.shape
    tiles, cells = capacity_ref.shape
    held_ref[...] = weight_ref[...].T
    total_ref[...] = jnp.zeros_like(total_ref)
    tile_iota = iota_bf((tiles, sources))
    cell_iota = iota_bf((cells, sources))

    def cover(first_row, stop_row):
        first = jnp.broadcast_to(first_row, cell_iota.shape)
        stop = jnp.broadcast_to(stop_row, cell_iota.shape)
        inside = jnp.logical_and(cell_iota >= first, cell_iota < stop)
        return jnp.where(inside, jnp.ones(cell_iota.shape, BF), jnp.zeros(cell_iota.shape, BF))

    def fields(base):
        tile_ids = to_bf(piece_ref[1, pl.ds(base, ROWS), :])
        first = piece_ref[2, pl.ds(base, ROWS), :]
        stop = first + piece_ref[3, pl.ds(base, ROWS), :]
        return tile_ids, first, stop

    def add(i, carry):
        base = pl.multiple_of(i * ROWS, ROWS)
        tile_ids, first, stop = fields(base)
        first, stop = to_bf(first), to_bf(stop)
        parts = split3(held_ref[pl.ds(base, ROWS), :])
        for j in range(0, ROWS, 2):
            lefts, rights = [], []
            for h in range(2):
                row = slice(j + h, j + h + 1)
                mask = tile_iota == jnp.broadcast_to(tile_ids[row], tile_iota.shape)
                lefts.append(
                    jnp.concatenate(
                        [
                            jnp.where(mask, jnp.broadcast_to(part[row], tile_iota.shape), jnp.zeros(tile_iota.shape, BF))
                            for part in parts
                        ],
                        axis=0,
                    )
                )
                rights.append(cover(first[row], stop[row]))
            total_ref[...] += lax.dot_general(
                jnp.concatenate(lefts, axis=1),
                jnp.concatenate(rights, axis=1),
                (((1,), (1,)), ((), ())),
                preferred_element_type=F32,
            )
        return carry

    lax.fori_loop(0, slots // ROWS, add, 0)
    demand = total_ref[:tiles] + total_ref[tiles : 2 * tiles] + total_ref[2 * tiles :]
    demand_ref[...] = demand
    pressure = jax.nn.sigmoid(SHARPNESS * (demand - capacity_ref[...].astype(F32)))
    table = jnp.concatenate(split3(pressure.T), axis=1)
    wide_iota = lax.broadcasted_iota(jnp.int32, (cells, sources), 0)

    def gather(i, carry):
        base = pl.multiple_of(i * ROWS, ROWS)
        tile_ids, first, stop = fields(base)
        rows = []
        for j in range(0, ROWS, 2):
            spread = []
            for h in range(2):
                hot = one_hot(tile_ids[j + h : j + h + 1], tile_iota)
                spread.append(jnp.concatenate([hot, hot, hot], axis=0))
            found = jnp.dot(table, jnp.concatenate(spread, axis=1), preferred_element_type=F32)
            for h in range(2):
                row = slice(j + h, j + h + 1)
                part = found[:, h * sources : (h + 1) * sources]
                inside = jnp.logical_and(wide_iota >= first[row], wide_iota < stop[row])
                rows.append(jnp.sum(jnp.where(inside, part, 0.0), axis=0, keepdims=True))
        back_ref[pl.ds(base, ROWS), :] = jnp.concatenate(rows, axis=0)
        return carry

    lax.fori_loop(0, slots // ROWS, gather, 0)
    grad_ref[...] = back_ref[...].T


def routes_kernel(grad_ref, send_ref, cost_ref, prob_ref, out_ref, held_ref, total_ref):
    cands, nets = prob_ref.shape
    slots, owners = send_ref.shape
    held_ref[...] = grad_ref[...].T
    total_ref[...] = jnp.zeros_like(total_ref)
    net_iota = iota_bf((nets, owners))
    cand_iota = iota_bf((cands, owners))

    def step(i, carry):
        base = pl.multiple_of(i * ROWS, ROWS)
        routes = send_ref[pl.ds(base, ROWS), :]
        net_ids = to_bf(lax.shift_right_arithmetic(routes, 5))
        cand_ids = to_bf(lax.bitwise_and(routes, 31))
        parts = split3(held_ref[pl.ds(base, ROWS), :])
        for j in range(0, ROWS, 2):
            lefts, rights = [], []
            for h in range(2):
                row = slice(j + h, j + h + 1)
                mask = cand_iota == jnp.broadcast_to(cand_ids[row], cand_iota.shape)
                lefts.append(
                    jnp.concatenate(
                        [
                            jnp.where(mask, jnp.broadcast_to(part[row], cand_iota.shape), jnp.zeros(cand_iota.shape, BF))
                            for part in parts
                        ],
                        axis=0,
                    )
                )
                rights.append(one_hot(net_ids[row], net_iota))
            total_ref[...] += lax.dot_general(
                jnp.concatenate(lefts, axis=1),
                jnp.concatenate(rights, axis=1),
                (((1,), (1,)), ((), ())),
                preferred_element_type=F32,
            )
        return carry

    lax.fori_loop(0, slots // ROWS, step, 0)
    probs = prob_ref[...]
    route_grad = cost_ref[...] + (total_ref[:cands] + total_ref[cands : 2 * cands] + total_ref[2 * cands :])
    expected = jnp.sum(probs * route_grad, axis=0, keepdims=True)
    out_ref[...] = probs * (route_grad - expected)


def in_vmem(count):
    return [pl.BlockSpec(memory_space=pltpu.VMEM)] * count


def body(logits, route_cost, capacity, send_route, recv_piece):
    nets, cands = logits.shape
    tiles, cells = capacity.shape
    send = send_route[0].T
    pieces = jnp.swapaxes(recv_piece[:, 0], 1, 2)
    slots, peers = send.shape
    pairs = jax.ShapeDtypeStruct((peers, slots), F32)
    by_slot = pltpu.VMEM((slots, peers), F32)
    weight, probs = pl.pallas_call(
        gather_kernel,
        out_shape=(pairs, jax.ShapeDtypeStruct((cands, nets), F32)),
        in_specs=in_vmem(2),
        out_specs=tuple(in_vmem(2)),
        scratch_shapes=[by_slot],
    )(logits.T, send)
    weight = lax.all_to_all(weight, "dev", split_axis=0, concat_axis=0, tiled=True)
    demand, slot_grad = pl.pallas_call(
        cells_kernel,
        out_shape=(jax.ShapeDtypeStruct((tiles, cells), F32), pairs),
        in_specs=in_vmem(3),
        out_specs=tuple(in_vmem(2)),
        scratch_shapes=[by_slot, pltpu.VMEM((3 * tiles, cells), F32), by_slot],
    )(weight, pieces, capacity)
    slot_grad = lax.all_to_all(slot_grad, "dev", split_axis=0, concat_axis=0, tiled=True)
    grad = pl.pallas_call(
        routes_kernel,
        out_shape=jax.ShapeDtypeStruct((cands, nets), F32),
        in_specs=in_vmem(4),
        out_specs=pl.BlockSpec(memory_space=pltpu.VMEM),
        scratch_shapes=[by_slot, pltpu.VMEM((3 * cands, nets), F32)],
    )(slot_grad, send, route_cost.T, probs)
    return demand, grad.T


def solution(mesh):
    placed = (
        P("dev", None),
        P("dev", None),
        P("dev", None),
        P("dev", None, None),
        P(None, "dev", None, None),
    )
    return jax.shard_map(
        body,
        mesh=mesh,
        in_specs=placed,
        out_specs=(P("dev", None), P("dev", None)),
        check_vma=False,
    )
```

time: 572 us -> 51.7 us (0.09); the launches traced: 565 us -> 51.4 us
  local copies, waits for them, and re-layouts: 312 us -> 0 us
  other arithmetic: 151 us -> 0 us
  waiting for transfers between devices: 78.5 us -> 0 us
  blocking collectives: 0 us -> 36.7 us
  Pallas kernels: 0 us -> 14.1 us
  between operations: 14.3 us -> 0.63 us
  starting transfers between devices: 9.16 us -> 0 us
    gather x5 -> x0, local copies, waits for them, and re-layouts: 306 us -> none  [the longest x1 215 us: body(): weight = everything[source_ids * route_total + route_in]]
    scatter-add x3 -> x0, other arithmetic: 147 us -> none  [the longest x1 51.9 us: body(): diff_marks.at[piece_stop.reshape(-1)].add(-weight.reshape(-1), mode='drop')]
    all_gather x1 -> x0, waiting for transfers between devices: 69.2 us -> none  [body(): everything = lax.all_gather(flat_probs, 'dev', axis=0, tiled=True)]
    all_to_all x0 -> x2, blocking collectives: none -> 36.7 us  [the longest x1 21.5 us: body(): lax.all_to_all(weight, 'dev', split_axis=0, concat_axis=0, tiled=True)]
    pallas_call x0 -> x3, Pallas kernels: none -> 14.1 us  [the longest x1 6.58 us: body(): pl.pallas_call(cells_kernel, out_shape=(jax.ShapeDtypeStruct((tiles, cell...]
    all_to_all x1 -> x0, waiting for transfers between devices: 9.34 us -> none  [body(): lax.all_to_all(slot_grad, 'dev', split_axis=0, concat_axis=0, tiled=True)]
    all_to_all x1 -> x0, starting transfers between devices: 9.12 us -> none  [body(): lax.all_to_all(slot_grad, 'dev', split_axis=0, concat_axis=0, tiled=True)]
  transfers between devices with their start and end apart: 2 -> 0, of which waited for: 2 -> 0; matrix products, arithmetic and copies ran while one was open for 1% -> 0% of each run, Pallas kernels for 0% -> 0%
where the time goes in v1:
time: 51.7 us; the launch traced here: 51.4 us
  blocking collectives  36.7 us (71%)
  Pallas kernels  14.1 us (27%)
  between operations  0.63 us (1%)
    all_to_all x1, blocking collectives, body(): lax.all_to_all(weight, 'dev', split_axis=0, concat_axis=0, tiled=True)  21.5 us
    all_to_all x1, blocking collectives, body(): lax.all_to_all(slot_grad, 'dev', split_axis=0, concat_axis=0, tiled=True)  15.2 us
    pallas_call x1, Pallas kernels, body(): pl.pallas_call(cells_kernel, out_shape=(jax.ShapeDtypeStruct((tiles, cell...  6.58 us
    pallas_call x1, Pallas kernels, body(): pl.pallas_call(routes_kernel, out_shape=jax.ShapeDtypeStruct((cands, nets...  4.01 us
    pallas_call x1, Pallas kernels, body(): pl.pallas_call(gather_kernel, out_shape=(pairs, jax.ShapeDtypeStruct((can...  3.48 us

profile of v1, /device:TPU:1, one launch (start us, length us, event | category | flops | bytes accessed | tf_op | source)
XLA Modules:
  0.0 51.4 jit_solution(8065703506957738069)
XLA Ops:
  0.6 3.5 %shard_map.68 = (f32[128,64]{1,0:T(8,128)}, f32[32,256]{1,0:T(8,128)}) custom-call(f32[32,256]{1,0:T(8,128)} %bitcast.24, s32[64,128]{1,0:T(8,128)} %bitcast.20), custom_call_target="tpu_custom_call" | custom-call | tf_op jit(solution)/shard_map/pallas_call | solution.py:202
  4.1 21.5 %all_to_all.22 = f32[128,1,64]{2,1,0:T(1,128)} all-to-all(f32[128,1,64]{2,1,0:T(1,128)} %bitcast.23), channel_id=1, replica_groups=mesh['dev'=128] {'dev'}, dimensions={0} | all-to-all | bytes 65536 | tf_op jit(solution)/shard_map/all_to_all | solution.py:209
  25.6 6.6 %shard_map.69 = (f32[64,128]{1,0:T(8,128)}, f32[128,64]{1,0:T(8,128)}) custom-call(f32[128,64]{1,0:T(8,128)} %bitcast.17, s32[4,64,128]{2,1,0:T(8,128)} %bitcast.19, s32[64,128]{1,0:T(8,128)} %capacity_ref.1), custom_call_target="tpu_custom_call" | custom-call | tf_op jit(solution)/shard_map/pallas_call | solution.py:210
  32.2 15.2 %all_to_all.23 = f32[128,1,64]{2,1,0:T(1,128)} all-to-all(f32[128,1,64]{2,1,0:T(1,128)} %bitcast.22), channel_id=1, replica_groups=mesh['dev'=128] {'dev'}, dimensions={0} | all-to-all | bytes 65536 | tf_op jit(solution)/shard_map/all_to_all | solution.py:217
  47.4 4.0 %shard_map.70 = f32[32,256]{1,0:T(8,128)} custom-call(f32[128,64]{1,0:T(8,128)} %bitcast.18, s32[64,128]{1,0:T(8,128)} %bitcast.21, f32[32,256]{1,0:T(8,128)} %bitcast.25, f32[32,256]{1,0:T(8,128)} %get-tuple-element.9.prob_ref), custom_call_target="tpu_custom_call" | custom-call | tf_op jit(solution)/shard_map/pallas_call | solution.py:218

commit v2 on v0

v2 whole, which is shorter than its diff:
```python
import jax
import jax.numpy as jnp
from jax import lax
from jax.experimental import pallas as pl
from jax.experimental.pallas import tpu as pltpu
from jax.sharding import PartitionSpec as P

SHARPNESS = 2.0
BF = jnp.bfloat16
F32 = jnp.float32
GATHER_ROWS = 32
CELL_ROWS = 32
ROUTE_ROWS = 64
PARAMS = pltpu.CompilerParams(vmem_limit_bytes=12 * 1024 * 1024)


def split(x):
    high = x.astype(BF)
    return high, (x - high.astype(F32)).astype(BF)


def iota(count, lanes):
    return lax.broadcasted_iota(jnp.int32, (count, lanes), 0)


def to_bf(x):
    return x.astype(F32).astype(BF)


def marks(mask):
    return jnp.where(mask, jnp.ones(mask.shape, BF), jnp.zeros(mask.shape, BF))


def hot(row, places):
    return places == jnp.broadcast_to(row, places.shape)


def spread(row, mask):
    return jnp.where(mask, jnp.broadcast_to(row, mask.shape), jnp.zeros(mask.shape, BF))


def pick(found, row, places):
    return jnp.sum(jnp.where(hot(row, places), found, 0.0), axis=0, keepdims=True)


def contract(left, right):
    return lax.dot_general(left, right, (((1,), (1,)), ((), ())), preferred_element_type=F32)


def route_places(routes, lanes):
    net = lax.shift_right_arithmetic(routes, 5)
    cand = lax.bitwise_and(routes, 31)
    column = lax.bitwise_and(net, lanes - 1)
    row = cand + 32 * lax.shift_right_arithmetic(net, 7)
    return column, row


def fold(x, lanes):
    return jnp.concatenate([x[:, i : i + lanes] for i in range(0, x.shape[1], lanes)], axis=0)


def unfold(x, rows):
    return jnp.concatenate([x[i : i + rows] for i in range(0, x.shape[0], rows)], axis=1)


def gather_kernel(logits_ref, send_ref, weight_ref, prob_ref, held_ref):
    slots, owners = send_ref.shape
    scores = logits_ref[...]
    powers = jnp.exp(scores - jnp.max(scores, axis=0, keepdims=True))
    probs = powers / jnp.sum(powers, axis=0, keepdims=True)
    prob_ref[...] = probs
    folded = fold(probs, owners)
    table = jnp.concatenate(split(folded), axis=1)
    columns = to_bf(iota(owners, owners))
    places = iota(folded.shape[0], owners)

    def step(i, carry):
        base = pl.multiple_of(i * GATHER_ROWS, GATHER_ROWS)
        column, row = route_places(send_ref[pl.ds(base, GATHER_ROWS), :], owners)
        column = to_bf(column)
        hots = jnp.concatenate([marks(hot(column[j : j + 1], columns)) for j in range(GATHER_ROWS)], axis=1)
        found = jnp.dot(table, jnp.concatenate([hots, hots], axis=0), preferred_element_type=F32)
        held_ref[pl.ds(base, GATHER_ROWS), :] = jnp.concatenate(
            [pick(found[:, j * owners : (j + 1) * owners], row[j : j + 1], places) for j in range(GATHER_ROWS)], axis=0
        )
        return carry

    lax.fori_loop(0, slots // GATHER_ROWS, step, 0)
    weight_ref[...] = held_ref[...].T


def cells_kernel(weight_ref, piece_ref, capacity_ref, demand_ref, grad_ref, held_ref, back_ref, cover_ref):
    slots, sources = held_ref.shape
    tiles, cells = capacity_ref.shape
    held_ref[...] = weight_ref[...].T
    tile_places = to_bf(iota(tiles, sources))
    cell_places = to_bf(iota(cells, sources))
    width = CELL_ROWS * sources

    def add(i, total):
        base = pl.multiple_of(i * CELL_ROWS, CELL_ROWS)
        tile = to_bf(piece_ref[1, pl.ds(base, CELL_ROWS), :])
        first = piece_ref[2, pl.ds(base, CELL_ROWS), :]
        stop = to_bf(first + piece_ref[3, pl.ds(base, CELL_ROWS), :])
        first = to_bf(first)
        parts = split(held_ref[pl.ds(base, CELL_ROWS), :])
        lefts, rights = [], []
        for j in range(CELL_ROWS):
            mask = hot(tile[j : j + 1], tile_places)
            lefts.append(jnp.concatenate([spread(part[j : j + 1], mask) for part in parts], axis=0))
            inside = jnp.logical_and(
                cell_places >= jnp.broadcast_to(first[j : j + 1], cell_places.shape),
                cell_places < jnp.broadcast_to(stop[j : j + 1], cell_places.shape),
            )
            rights.append(marks(inside))
        right = jnp.concatenate(rights, axis=1)
        cover_ref[:, pl.ds(pl.multiple_of(i * width, width), width)] = right
        return total + contract(jnp.concatenate(lefts, axis=1), right)

    total = lax.fori_loop(0, slots // CELL_ROWS, add, jnp.zeros((2 * tiles, cells), F32))
    demand = total[:tiles] + total[tiles:]
    demand_ref[...] = demand
    pressure = jax.nn.sigmoid(SHARPNESS * (demand - capacity_ref[...].astype(F32)))
    table = jnp.concatenate(split(pressure), axis=1)
    places = iota(tiles, sources)

    def gather(i, carry):
        base = pl.multiple_of(i * CELL_ROWS, CELL_ROWS)
        tile = piece_ref[1, pl.ds(base, CELL_ROWS), :]
        cover = cover_ref[:, pl.ds(pl.multiple_of(i * width, width), width)]
        found = jnp.dot(table, jnp.concatenate([cover, cover], axis=0), preferred_element_type=F32)
        back_ref[pl.ds(base, CELL_ROWS), :] = jnp.concatenate(
            [pick(found[:, j * sources : (j + 1) * sources], tile[j : j + 1], places) for j in range(CELL_ROWS)], axis=0
        )
        return carry

    lax.fori_loop(0, slots // CELL_ROWS, gather, 0)
    grad_ref[...] = back_ref[...].T


def routes_kernel(grad_ref, send_ref, cost_ref, prob_ref, out_ref, held_ref):
    cands, nets = prob_ref.shape
    slots, owners = send_ref.shape
    rows = cands * nets // owners
    held_ref[...] = grad_ref[...].T
    columns = to_bf(iota(owners, owners))
    places = to_bf(iota(rows, owners))

    def step(i, total):
        base = pl.multiple_of(i * ROUTE_ROWS, ROUTE_ROWS)
        column, row = route_places(send_ref[pl.ds(base, ROUTE_ROWS), :], owners)
        column, row = to_bf(column), to_bf(row)
        parts = split(held_ref[pl.ds(base, ROUTE_ROWS), :])
        lefts, rights = [], []
        for j in range(ROUTE_ROWS):
            mask = hot(row[j : j + 1], places)
            lefts.append(jnp.concatenate([spread(part[j : j + 1], mask) for part in parts], axis=0))
            rights.append(marks(hot(column[j : j + 1], columns)))
        return total + contract(jnp.concatenate(lefts, axis=1), jnp.concatenate(rights, axis=1))

    total = lax.fori_loop(0, slots // ROUTE_ROWS, step, jnp.zeros((2 * rows, owners), F32))
    probs = prob_ref[...]
    route_grad = cost_ref[...] + unfold(total[:rows] + total[rows:], cands)
    expected = jnp.sum(probs * route_grad, axis=0, keepdims=True)
    out_ref[...] = probs * (route_grad - expected)


def in_vmem(count):
    return [pl.BlockSpec(memory_space=pltpu.VMEM)] * count


def gather_call(logits, send):
    cands, nets = logits.shape
    slots, peers = send.shape
    return pl.pallas_call(
        gather_kernel,
        out_shape=(jax.ShapeDtypeStruct((peers, slots), F32), jax.ShapeDtypeStruct((cands, nets), F32)),
        in_specs=in_vmem(2),
        out_specs=tuple(in_vmem(2)),
        compiler_params=PARAMS,
        scratch_shapes=[pltpu.VMEM((slots, peers), F32)],
    )(logits, send)


def cells_call(weight, pieces, capacity):
    tiles, cells = capacity.shape
    peers, slots = weight.shape
    by_slot = pltpu.VMEM((slots, peers), F32)
    return pl.pallas_call(
        cells_kernel,
        out_shape=(jax.ShapeDtypeStruct((tiles, cells), F32), jax.ShapeDtypeStruct((peers, slots), F32)),
        in_specs=in_vmem(3),
        out_specs=tuple(in_vmem(2)),
        compiler_params=PARAMS,
        scratch_shapes=[by_slot, by_slot, pltpu.VMEM((cells, slots * peers), BF)],
    )(weight, pieces, capacity)


def routes_call(slot_grad, send, route_cost, probs):
    return pl.pallas_call(
        routes_kernel,
        out_shape=jax.ShapeDtypeStruct(probs.shape, F32),
        in_specs=in_vmem(4),
        out_specs=pl.BlockSpec(memory_space=pltpu.VMEM),
        compiler_params=PARAMS,
        scratch_shapes=[pltpu.VMEM(send.shape, F32)],
    )(slot_grad, send, route_cost, probs)


def exchange(x):
    return lax.all_to_all(x, "dev", split_axis=0, concat_axis=0, tiled=True)


def body(logits, route_cost, capacity, send_route, recv_piece):
    send = send_route[0].T
    pieces = jnp.swapaxes(recv_piece[:, 0], 1, 2)
    weight, probs = gather_call(logits.T, send)
    demand, slot_grad = cells_call(exchange(weight), pieces, capacity)
    grad = routes_call(exchange(slot_grad), send, route_cost.T, probs)
    return demand, grad.T


def solution(mesh):
    placed = (
        P("dev", None),
        P("dev", None),
        P("dev", None),
        P("dev", None, None),
        P(None, "dev", None, None),
    )
    return jax.shard_map(
        body,
        mesh=mesh,
        in_specs=placed,
        out_specs=(P("dev", None), P("dev", None)),
        check_vma=False,
    )
```

time: 572 us -> 42.1 us (0.07); the launches traced: 565 us -> 41.7 us
  local copies, waits for them, and re-layouts: 312 us -> 1.56 us
  other arithmetic: 151 us -> 0 us
  waiting for transfers between devices: 78.5 us -> 0 us
  blocking collectives: 0 us -> 34.8 us
  between operations: 14.3 us -> 0.67 us
  starting transfers between devices: 9.16 us -> 0 us
    gather x5 -> x0, local copies, waits for them, and re-layouts: 306 us -> none  [the longest x1 215 us: body(): weight = everything[source_ids * route_total + route_in]]
    scatter-add x3 -> x0, other arithmetic: 147 us -> none  [the longest x1 51.9 us: body(): diff_marks.at[piece_stop.reshape(-1)].add(-weight.reshape(-1), mode='drop')]
    all_gather x1 -> x0, waiting for transfers between devices: 69.2 us -> none  [body(): everything = lax.all_gather(flat_probs, 'dev', axis=0, tiled=True)]
    all_to_all x0 -> x2, blocking collectives: none -> 34.8 us  [exchange(): return lax.all_to_all(x, 'dev', split_axis=0, concat_axis=0, tiled=True)]
    all_to_all x1 -> x0, waiting for transfers between devices: 9.34 us -> none  [body(): lax.all_to_all(slot_grad, 'dev', split_axis=0, concat_axis=0, tiled=True)]
    all_to_all x1 -> x0, starting transfers between devices: 9.12 us -> none  [body(): lax.all_to_all(slot_grad, 'dev', split_axis=0, concat_axis=0, tiled=True)]
  transfers between devices with their start and end apart: 2 -> 0, of which waited for: 2 -> 0; matrix products, arithmetic and copies ran while one was open for 1% -> 0% of each run, Pallas kernels for 0% -> 0%
where the time goes in v2:
time: 42.1 us; the launch traced here: 41.7 us
  blocking collectives  34.8 us (83%)
  Pallas kernels  4.69 us (11%)
  local copies, waits for them, and re-layouts  1.56 us (4%)
  between operations  0.67 us (2%)
    all_to_all x2, blocking collectives, exchange(): return lax.all_to_all(x, 'dev', split_axis=0, concat_axis=0, tiled=True)  34.8 us
    pallas_call x1, Pallas kernels, cells_call(): pl.pallas_call(cells_kernel, out_shape=(jax.ShapeDtypeStruct((tiles, cell...  2.15 us
    unnamed x12, local copies, waits for them, and re-layouts  1.56 us
    pallas_call x1, Pallas kernels, routes_call(): pl.pallas_call(routes_kernel, out_shape=jax.ShapeDtypeStruct(probs.shape,...  1.4 us
    pallas_call x1, Pallas kernels, gather_call(): pl.pallas_call(gather_kernel, out_shape=(jax.ShapeDtypeStruct((peers, slo...  1.14 us

profile of v2, /device:TPU:1, one launch (start us, length us, event | category | flops | bytes accessed | tf_op | source)
XLA Modules:
  0.0 41.7 jit_solution(9413007837531897052)
XLA Ops:
  0.6 0.0 copy-start
  0.6 0.0 copy-start.1
  0.7 0.8 %copy-done.1 = s32[1,128,64]{1,2,0:T(8,128)S(1)} copy-done((s32[1,128,64]{1,2,0:T(8,128)S(1)}, s32[1,128,64]{1,2,0:T(8,128)}, u32[]{:S(2)}) %copy-start.1) | copy-done | bytes 32792
  1.4 0.0 copy-start.4
  1.4 0.8 %copy-done.4 = f32[256,32]{0,1:T(8,128)S(1)} copy-done((f32[256,32]{0,1:T(8,128)S(1)}, f32[256,32]{0,1:T(8,128)}, u32[]{:S(2)}) %copy-start.4) | copy-done | bytes 32792
  2.2 1.1 %shard_map.68 = (f32[128,64]{1,0:T(8,128)S(1)}, f32[32,256]{1,0:T(8,128)S(1)}) custom-call(f32[32,256]{1,0:T(8,128)S(1)} %bitcast.24, s32[64,128]{1,0:T(8,128)S(1)} %bitcast.20), custom_call_target="tpu_custom_call" | custom-call | tf_op jit(solution)/shard_map/pallas_call | solution.py:175
  3.3 0.0 copy-start.3
  3.3 20.9 %all_to_all.22 = f32[128,1,64]{2,1,0:T(1,128)S(1)} all-to-all(f32[128,1,64]{2,1,0:T(1,128)S(1)} %bitcast.23), channel_id=1, replica_groups=mesh['dev'=128] {'dev'}, dimensions={0} | all-to-all | bytes 65536 | tf_op jit(solution)/shard_map/all_to_all | solution.py:211
  24.3 0.0 copy-done
  24.3 0.0 copy-done.3
  24.3 2.2 %shard_map.69 = (f32[64,128]{1,0:T(8,128)}, f32[128,64]{1,0:T(8,128)S(1)}) custom-call(f32[128,64]{1,0:T(8,128)S(1)} %bitcast.17, s32[4,64,128]{2,1,0:T(8,128)S(1)} %bitcast.19, s32[64,128]{1,0:T(8,128)S(1)} %copy-done.3), custom_call_target="tpu_custom_call" | custom-call | tf_op jit(solution)/shard_map/pallas_call | solution.py:189
  26.4 0.0 copy-start.2
  26.4 0.0 copy-start.5
  26.4 13.9 %all_to_all.23 = f32[128,1,64]{2,1,0:T(1,128)S(1)} all-to-all(f32[128,1,64]{2,1,0:T(1,128)S(1)} %bitcast.22), channel_id=1, replica_groups=mesh['dev'=128] {'dev'}, dimensions={0} | all-to-all | bytes 65536 | tf_op jit(solution)/shard_map/all_to_all | solution.py:211
  40.3 0.0 copy-done.2
  40.3 0.0 copy-done.5
  40.3 1.4 %shard_map.70 = f32[32,256]{1,0:T(8,128)} custom-call(f32[128,64]{1,0:T(8,128)S(1)} %bitcast.18, s32[64,128]{1,0:T(8,128)S(1)} %bitcast.21, f32[32,256]{1,0:T(8,128)S(1)} %bitcast.25, f32[32,256]{1,0:T(8,128)S(1)} %get-tuple-element.9.prob_ref), custom_call_target="tpu_custom_call" | custom-call | tf_op jit(solution)/shard_map/pallas_call | solution.py:200
Async XLA Ops:
  0.6 23.6 %copy-start = (s32[4,1,128,64]{2,3,1,0:T(8,128)S(1)}, s32[4,1,128,64]{2,3,1,0:T(8,128)}, u32[]{:S(2)}) copy-start(s32[4,1,128,64]{2,3,1,0:T(8,128)} %param.9) | copy-start | bytes 393220
  0.6 0.8 %copy-start.1 = (s32[1,128,64]{1,2,0:T(8,128)S(1)}, s32[1,128,64]{1,2,0:T(8,128)}, u32[]{:S(2)}) copy-start(s32[1,128,64]{1,2,0:T(8,128)} %param.8) | copy-start | bytes 98308
  1.4 0.8 %copy-start.4 = (f32[256,32]{0,1:T(8,128)S(1)}, f32[256,32]{0,1:T(8,128)}, u32[]{:S(2)}) copy-start(f32[256,32]{0,1:T(8,128)} %param.5) | copy-start | bytes 98308
  3.3 20.9 %copy-start.3 = (s32[64,128]{1,0:T(8,128)S(1)}, s32[64,128]{1,0:T(8,128)}, u32[]{:S(2)}) copy-start(s32[64,128]{1,0:T(8,128)} %capacity_ref.1) | copy-start | bytes 98308
  26.4 13.9 %copy-start.2 = (s32[1,128,64]{1,2,0:T(8,128)S(1)}, s32[1,128,64]{1,2,0:T(8,128)}, u32[]{:S(2)}) copy-start(s32[1,128,64]{1,2,0:T(8,128)} %param.8) | copy-start | bytes 98308
  26.4 13.9 %copy-start.5 = (f32[256,32]{0,1:T(8,128)S(1)}, f32[256,32]{0,1:T(8,128)}, u32[]{:S(2)}) copy-start(f32[256,32]{0,1:T(8,128)} %param.6) | copy-start | bytes 98308

commit v3 on v2

--- a/solution.py
+++ b/solution.py
@@ -8,8 +8,13 @@
 SHARPNESS = 2.0
 BF = jnp.bfloat16
 F32 = jnp.float32
-GATHER_ROWS = 32
-CELL_ROWS = 32
+CELL_DOT = 64
+CELL_BACK = 4
+CELL_BACK_ROWS = 32
+CELL_STACK = 1
+ROUTE_DOT = 64
+SUBLANES = 8
+CELL_ROWS = 64
 ROUTE_ROWS = 64
 PARAMS = pltpu.CompilerParams(vmem_limit_bytes=12 * 1024 * 1024)
 
@@ -63,33 +68,40 @@
     return jnp.concatenate([x[i : i + rows] for i in range(0, x.shape[0], rows)], axis=1)
 
 
-def gather_kernel(logits_ref, send_ref, weight_ref, prob_ref, held_ref):
+def gather_kernel(logits_hbm, send_hbm, weight_ref, prob_ref, logits_ref, send_ref, table_ref, held_ref, sems):
     slots, owners = send_ref.shape
+    scores_in = pltpu.make_async_copy(logits_hbm, logits_ref, sems.at[0])
+    routes_in = pltpu.make_async_copy(send_hbm, send_ref, sems.at[1])
+    scores_in.start()
+    routes_in.start()
+    scores_in.wait()
     scores = logits_ref[...]
     powers = jnp.exp(scores - jnp.max(scores, axis=0, keepdims=True))
     probs = powers / jnp.sum(powers, axis=0, keepdims=True)
     prob_ref[...] = probs
-    folded = fold(probs, owners)
-    table = jnp.concatenate(split(folded), axis=1)
-    columns = to_bf(iota(owners, owners))
-    places = iota(folded.shape[0], owners)
-
-    def step(i, carry):
-        base = pl.multiple_of(i * GATHER_ROWS, GATHER_ROWS)
-        column, row = route_places(send_ref[pl.ds(base, GATHER_ROWS), :], owners)
-        column = to_bf(column)
-        hots = jnp.concatenate([marks(hot(column[j : j + 1], columns)) for j in range(GATHER_ROWS)], axis=1)
-        found = jnp.dot(table, jnp.concatenate([hots, hots], axis=0), preferred_element_type=F32)
-        held_ref[pl.ds(base, GATHER_ROWS), :] = jnp.concatenate(
-            [pick(found[:, j * owners : (j + 1) * owners], row[j : j + 1], places) for j in range(GATHER_ROWS)], axis=0
-        )
-        return carry
-
-    lax.fori_loop(0, slots // GATHER_ROWS, step, 0)
+    table_ref[...] = fold(probs, owners)
+    routes_in.wait()
+    column, row = route_places(send_ref[...], owners)
+    blocks = range(0, slots, SUBLANES)
+    shape = (SUBLANES, owners)
+    columns = [column[i : i + SUBLANES] for i in blocks]
+    rows = [row[i : i + SUBLANES] for i in blocks]
+
+    def take(t, n, found):
+        entries = jnp.broadcast_to(table_ref[t : t + 1, :], shape)
+        entries = jnp.take_along_axis(entries, columns[n], axis=1, mode="promise_in_bounds")
+        return jnp.where(rows[n] == t, entries, found)
+
+    founds = [jnp.zeros(shape, F32) for _ in blocks]
+    for n in range(len(founds)):
+        for t in range(table_ref.shape[0]):
+            founds[n] = take(t, n, founds[n])
+    for n, i in enumerate(blocks):
+        held_ref[i : i + SUBLANES, :] = founds[n]
     weight_ref[...] = held_ref[...].T
 
 
-def cells_kernel(weight_ref, piece_ref, capacity_ref, demand_ref, grad_ref, held_ref, back_ref, cover_ref):
+def cells_kernel(weight_ref, piece_ref, capacity_ref, demand_hbm, grad_ref, held_ref, back_ref, cover_ref, demand_ref, sem):
     slots, sources = held_ref.shape
     tiles, cells = capacity_ref.shape
     held_ref[...] = weight_ref[...].T
@@ -104,38 +116,47 @@
         stop = to_bf(first + piece_ref[3, pl.ds(base, CELL_ROWS), :])
         first = to_bf(first)
         parts = split(held_ref[pl.ds(base, CELL_ROWS), :])
-        lefts, rights = [], []
-        for j in range(CELL_ROWS):
-            mask = hot(tile[j : j + 1], tile_places)
-            lefts.append(jnp.concatenate([spread(part[j : j + 1], mask) for part in parts], axis=0))
-            inside = jnp.logical_and(
-                cell_places >= jnp.broadcast_to(first[j : j + 1], cell_places.shape),
-                cell_places < jnp.broadcast_to(stop[j : j + 1], cell_places.shape),
-            )
-            rights.append(marks(inside))
-        right = jnp.concatenate(rights, axis=1)
-        cover_ref[:, pl.ds(pl.multiple_of(i * width, width), width)] = right
-        return total + contract(jnp.concatenate(lefts, axis=1), right)
+        for k in range(0, CELL_ROWS, CELL_DOT):
+            lefts, rights = [], []
+            for j in range(k, k + CELL_DOT):
+                mask = hot(tile[j : j + 1], tile_places)
+                lefts.append(jnp.concatenate([spread(part[j : j + 1], mask) for part in parts], axis=0))
+                inside = jnp.logical_and(
+                    cell_places >= jnp.broadcast_to(first[j : j + 1], cell_places.shape),
+                    cell_places < jnp.broadcast_to(stop[j : j + 1], cell_places.shape),
+                )
+                rights.append(marks(inside))
+                cover_ref[:, pl.ds(pl.multiple_of(i * width + j * sources, sources), sources)] = rights[-1]
+            total = total + contract(jnp.concatenate(lefts, axis=1), jnp.concatenate(rights, axis=1))
+        return total
 
     total = lax.fori_loop(0, slots // CELL_ROWS, add, jnp.zeros((2 * tiles, cells), F32))
     demand = total[:tiles] + total[tiles:]
     demand_ref[...] = demand
+    demand_out = pltpu.make_async_copy(demand_ref, demand_hbm, sem)
+    demand_out.start()
     pressure = jax.nn.sigmoid(SHARPNESS * (demand - capacity_ref[...].astype(F32)))
-    table = jnp.concatenate(split(pressure), axis=1)
+    table = jnp.concatenate(split(pressure), axis=1 - CELL_STACK)
     places = iota(tiles, sources)
 
     def gather(i, carry):
-        base = pl.multiple_of(i * CELL_ROWS, CELL_ROWS)
-        tile = piece_ref[1, pl.ds(base, CELL_ROWS), :]
-        cover = cover_ref[:, pl.ds(pl.multiple_of(i * width, width), width)]
-        found = jnp.dot(table, jnp.concatenate([cover, cover], axis=0), preferred_element_type=F32)
-        back_ref[pl.ds(base, CELL_ROWS), :] = jnp.concatenate(
-            [pick(found[:, j * sources : (j + 1) * sources], tile[j : j + 1], places) for j in range(CELL_ROWS)], axis=0
-        )
+        base = pl.multiple_of(i * CELL_BACK_ROWS, CELL_BACK_ROWS)
+        tile = piece_ref[1, pl.ds(base, CELL_BACK_ROWS), :]
+        picked = []
+        for k in range(0, CELL_BACK_ROWS, CELL_BACK):
+            cover = cover_ref[:, pl.ds(pl.multiple_of((base + k) * sources, sources), CELL_BACK * sources)]
+            if CELL_STACK:
+                found = jnp.dot(table, cover, preferred_element_type=F32)
+                found = found[:tiles] + found[tiles:]
+            else:
+                found = jnp.dot(table, jnp.concatenate([cover, cover], axis=0), preferred_element_type=F32)
+            picked += [pick(found[:, (j - k) * sources : (j - k + 1) * sources], tile[j : j + 1], places) for j in range(k, k + CELL_BACK)]
+        back_ref[pl.ds(base, CELL_BACK_ROWS), :] = jnp.concatenate(picked, axis=0)
         return carry
 
-    lax.fori_loop(0, slots // CELL_ROWS, gather, 0)
+    lax.fori_loop(0, slots // CELL_BACK_ROWS, gather, 0)
     grad_ref[...] = back_ref[...].T
+    demand_out.wait()
 
 
 def routes_kernel(grad_ref, send_ref, cost_ref, prob_ref, out_ref, held_ref):
@@ -151,12 +172,14 @@
         column, row = route_places(send_ref[pl.ds(base, ROUTE_ROWS), :], owners)
         column, row = to_bf(column), to_bf(row)
         parts = split(held_ref[pl.ds(base, ROUTE_ROWS), :])
-        lefts, rights = [], []
-        for j in range(ROUTE_ROWS):
-            mask = hot(row[j : j + 1], places)
-            lefts.append(jnp.concatenate([spread(part[j : j + 1], mask) for part in parts], axis=0))
-            rights.append(marks(hot(column[j : j + 1], columns)))
-        return total + contract(jnp.concatenate(lefts, axis=1), jnp.concatenate(rights, axis=1))
+        for k in range(0, ROUTE_ROWS, ROUTE_DOT):
+            lefts, rights = [], []
+            for j in range(k, k + ROUTE_DOT):
+                mask = hot(row[j : j + 1], places)
+                lefts.append(jnp.concatenate([spread(part[j : j + 1], mask) for part in parts], axis=0))
+                rights.append(marks(hot(column[j : j + 1], columns)))
+            total = total + contract(jnp.concatenate(lefts, axis=1), jnp.concatenate(rights, axis=1))
+        return total
 
     total = lax.fori_loop(0, slots // ROUTE_ROWS, step, jnp.zeros((2 * rows, owners), F32))
     probs = prob_ref[...]
@@ -167,6 +190,10 @@
 
 def in_vmem(count):
     return [pl.BlockSpec(memory_space=pltpu.VMEM)] * count
+
+
+def in_hbm(count):
+    return [pl.BlockSpec(memory_space=pltpu.HBM)] * count
 
 
 def gather_call(logits, send):
@@ -175,10 +202,16 @@
     return pl.pallas_call(
         gather_kernel,
         out_shape=(jax.ShapeDtypeStruct((peers, slots), F32), jax.ShapeDtypeStruct((cands, nets), F32)),
-        in_specs=in_vmem(2),
+        in_specs=in_hbm(2),
         out_specs=tuple(in_vmem(2)),
         compiler_params=PARAMS,
-        scratch_shapes=[pltpu.VMEM((slots, peers), F32)],
+        scratch_shapes=[
+            pltpu.VMEM((cands, nets), F32),
+            pltpu.VMEM((slots, peers), jnp.int32),
+            pltpu.VMEM((cands * nets // peers, peers), F32),
+            pltpu.VMEM((slots, peers), F32),
+            pltpu.SemaphoreType.DMA((2,)),
+        ],
     )(logits, send)
 
 
@@ -190,9 +223,15 @@
         cells_kernel,
         out_shape=(jax.ShapeDtypeStruct((tiles, cells), F32), jax.ShapeDtypeStruct((peers, slots), F32)),
         in_specs=in_vmem(3),
-        out_specs=tuple(in_vmem(2)),
+        out_specs=tuple(in_hbm(1) + in_vmem(1)),
         compiler_params=PARAMS,
-        scratch_shapes=[by_slot, by_slot, pltpu.VMEM((cells, slots * peers), BF)],
+        scratch_shapes=[
+            by_slot,
+            by_slot,
+            pltpu.VMEM((cells, slots * peers), BF),
+            pltpu.VMEM((tiles, cells), F32),
+            pltpu.SemaphoreType.DMA,
+        ],
     )(weight, pieces, capacity)
 
 

time: 42.1 us -> 41.4 us (0.983)
  Pallas kernels: 4.69 us -> 4.01 us
where the time goes in v3:
time: 41.4 us; the launch traced here: 41.1 us
  blocking collectives  34.8 us (84%)
  Pallas kernels  4.01 us (10%)
  local copies, waits for them, and re-layouts  1.57 us (4%)
  between operations  0.69 us (2%)
    all_to_all x2, blocking collectives, exchange(): return lax.all_to_all(x, 'dev', split_axis=0, concat_axis=0, tiled=True)  34.8 us
    pallas_call x1, Pallas kernels, cells_call(): pl.pallas_call(cells_kernel, out_shape=(jax.ShapeDtypeStruct((tiles, cell...  1.79 us
    unnamed x12, local copies, waits for them, and re-layouts  1.57 us
    pallas_call x1, Pallas kernels, routes_call(): pl.pallas_call(routes_kernel, out_shape=jax.ShapeDtypeStruct(probs.shape,...  1.39 us
    pallas_call x1, Pallas kernels, gather_call(): pl.pallas_call(gather_kernel, out_shape=(jax.ShapeDtypeStruct((peers, slo...  0.83 us

profile of v3, /device:TPU:1, one launch (start us, length us, event | category | flops | bytes accessed | tf_op | source)
XLA Modules:
  0.0 41.1 jit_solution(9645200088434238021)
XLA Ops:
  0.6 0.0 copy-start
  0.6 0.0 copy-start.1
  0.7 0.8 %copy-done.1 = s32[1,128,64]{1,2,0:T(8,128)S(1)} copy-done((s32[1,128,64]{1,2,0:T(8,128)S(1)}, s32[1,128,64]{1,2,0:T(8,128)}, u32[]{:S(2)}) %copy-start.1) | copy-done | bytes 32792
  1.4 0.0 copy-start.4
  1.4 0.8 %copy-done.4 = f32[256,32]{0,1:T(8,128)S(1)} copy-done((f32[256,32]{0,1:T(8,128)S(1)}, f32[256,32]{0,1:T(8,128)}, u32[]{:S(2)}) %copy-start.4) | copy-done | bytes 32792
  2.2 0.8 %shard_map.68 = (f32[128,64]{1,0:T(8,128)S(1)}, f32[32,256]{1,0:T(8,128)S(1)}) custom-call(f32[32,256]{1,0:T(8,128)S(1)} %bitcast.24, s32[64,128]{1,0:T(8,128)S(1)} %bitcast.20), custom_call_target="tpu_custom_call" | custom-call | tf_op jit(solution)/shard_map/pallas_call | solution.py:202
  3.0 0.0 copy-start.3
  3.0 20.9 %all_to_all.22 = f32[128,1,64]{2,1,0:T(1,128)S(1)} all-to-all(f32[128,1,64]{2,1,0:T(1,128)S(1)} %bitcast.23), channel_id=1, replica_groups=mesh['dev'=128] {'dev'}, dimensions={0} | all-to-all | bytes 65536 | tf_op jit(solution)/shard_map/all_to_all | solution.py:250
  24.0 0.0 copy-done
  24.0 0.0 copy-done.3
  24.0 1.8 %shard_map.69 = (f32[64,128]{1,0:T(8,128)}, f32[128,64]{1,0:T(8,128)S(1)}) custom-call(f32[128,64]{1,0:T(8,128)S(1)} %bitcast.17, s32[4,64,128]{2,1,0:T(8,128)S(1)} %bitcast.19, s32[64,128]{1,0:T(8,128)S(1)} %copy-done.3), custom_call_target="tpu_custom_call" | custom-call | tf_op jit(solution)/shard_map/pallas_call | solution.py:222
  25.8 0.0 copy-start.2
  25.8 0.0 copy-start.5
  25.8 13.9 %all_to_all.23 = f32[128,1,64]{2,1,0:T(1,128)S(1)} all-to-all(f32[128,1,64]{2,1,0:T(1,128)S(1)} %bitcast.22), channel_id=1, replica_groups=mesh['dev'=128] {'dev'}, dimensions={0} | all-to-all | bytes 65536 | tf_op jit(solution)/shard_map/all_to_all | solution.py:250
  39.7 0.0 copy-done.2
  39.7 0.0 copy-done.5
  39.7 1.4 %shard_map.70 = f32[32,256]{1,0:T(8,128)} custom-call(f32[128,64]{1,0:T(8,128)S(1)} %bitcast.18, s32[64,128]{1,0:T(8,128)S(1)} %bitcast.21, f32[32,256]{1,0:T(8,128)S(1)} %bitcast.25, f32[32,256]{1,0:T(8,128)S(1)} %get-tuple-element.9.prob_ref), custom_call_target="tpu_custom_call" | custom-call | tf_op jit(solution)/shard_map/pallas_call | solution.py:239
Async XLA Ops:
  0.6 23.3 %copy-start = (s32[4,1,128,64]{2,3,1,0:T(8,128)S(1)}, s32[4,1,128,64]{2,3,1,0:T(8,128)}, u32[]{:S(2)}) copy-start(s32[4,1,128,64]{2,3,1,0:T(8,128)} %param.9) | copy-start | bytes 393220
  0.6 0.8 %copy-start.1 = (s32[1,128,64]{1,2,0:T(8,128)S(1)}, s32[1,128,64]{1,2,0:T(8,128)}, u32[]{:S(2)}) copy-start(s32[1,128,64]{1,2,0:T(8,128)} %param.8) | copy-start | bytes 98308
  1.4 0.8 %copy-start.4 = (f32[256,32]{0,1:T(8,128)S(1)}, f32[256,32]{0,1:T(8,128)}, u32[]{:S(2)}) copy-start(f32[256,32]{0,1:T(8,128)} %param.5) | copy-start | bytes 98308
  3.0 20.9 %copy-start.3 = (s32[64,128]{1,0:T(8,128)S(1)}, s32[64,128]{1,0:T(8,128)}, u32[]{:S(2)}) copy-start(s32[64,128]{1,0:T(8,128)} %capacity_ref.1) | copy-start | bytes 98308
  25.8 13.9 %copy-start.2 = (s32[1,128,64]{1,2,0:T(8,128)S(1)}, s32[1,128,64]{1,2,0:T(8,128)}, u32[]{:S(2)}) copy-start(s32[1,128,64]{1,2,0:T(8,128)} %param.8) | copy-start | bytes 98308
  25.8 13.9 %copy-start.5 = (f32[256,32]{0,1:T(8,128)S(1)}, f32[256,32]{0,1:T(8,128)}, u32[]{:S(2)}) copy-start(f32[256,32]{0,1:T(8,128)} %param.6) | copy-start | bytes 98308

commit v4 on v3

--- a/solution.py
+++ b/solution.py
@@ -212,7 +212,7 @@
             pltpu.VMEM((slots, peers), F32),
             pltpu.SemaphoreType.DMA((2,)),
         ],
-    )(logits, send)
+    )(*[pltpu.with_memory_space_constraint(x, pltpu.HBM) for x in (logits, send)])
 
 
 def cells_call(weight, pieces, capacity):

time: 41.4 us -> 40.6 us (0.981)
  local copies, waits for them, and re-layouts: 1.57 us -> 0.02 us
  Pallas kernels: 4.01 us -> 4.76 us
    unnamed x12 -> x8, local copies, waits for them, and re-layouts: 1.57 us -> 0.02 us
    pallas_call x1, Pallas kernels: 0.83 us -> 1.57 us  [gather_call(): pl.pallas_call(gather_kernel, out_shape=(jax.ShapeDtypeStruct((peers, slo...]
where the time goes in v4:
time: 40.6 us; the launch traced here: 40.3 us
  blocking collectives  34.8 us (86%)
  Pallas kernels  4.76 us (12%)
  between operations  0.68 us (2%)
    all_to_all x2, blocking collectives, exchange(): return lax.all_to_all(x, 'dev', split_axis=0, concat_axis=0, tiled=True)  34.8 us
    pallas_call x1, Pallas kernels, cells_call(): pl.pallas_call(cells_kernel, out_shape=(jax.ShapeDtypeStruct((tiles, cell...  1.79 us
    pallas_call x1, Pallas kernels, gather_call(): pl.pallas_call(gather_kernel, out_shape=(jax.ShapeDtypeStruct((peers, slo...  1.57 us
    pallas_call x1, Pallas kernels, routes_call(): pl.pallas_call(routes_kernel, out_shape=jax.ShapeDtypeStruct(probs.shape,...  1.4 us

profile of v4, /device:TPU:1, one launch (start us, length us, event | category | flops | bytes accessed | tf_op | source)
XLA Modules:
  0.0 40.3 jit_solution(18163132163903987749)
XLA Ops:
  0.6 0.0 copy-start
  0.6 1.6 %shard_map.68 = (f32[128,64]{1,0:T(8,128)S(1)}, f32[32,256]{1,0:T(8,128)S(1)}) custom-call(f32[32,256]{1,0:T(8,128)} %bitcast.25, s32[64,128]{1,0:T(8,128)} %bitcast.20), custom_call_target="tpu_custom_call" | custom-call | tf_op jit(solution)/shard_map/pallas_call | solution.py:202
  2.2 0.0 copy-start.2
  2.2 20.9 %all_to_all.22 = f32[128,1,64]{2,1,0:T(1,128)S(1)} all-to-all(f32[128,1,64]{2,1,0:T(1,128)S(1)} %bitcast.23), channel_id=1, replica_groups=mesh['dev'=128] {'dev'}, dimensions={0} | all-to-all | bytes 65536 | tf_op jit(solution)/shard_map/all_to_all | solution.py:250
  23.1 0.0 copy-done
  23.1 0.0 copy-done.2
  23.2 1.8 %shard_map.69 = (f32[64,128]{1,0:T(8,128)}, f32[128,64]{1,0:T(8,128)S(1)}) custom-call(f32[128,64]{1,0:T(8,128)S(1)} %bitcast.17, s32[4,64,128]{2,1,0:T(8,128)S(1)} %bitcast.19, s32[64,128]{1,0:T(8,128)S(1)} %copy-done.2), custom_call_target="tpu_custom_call" | custom-call | tf_op jit(solution)/shard_map/pallas_call | solution.py:222
  24.9 0.0 copy-start.1
  25.0 0.0 copy-start.3
  25.0 13.9 %all_to_all.23 = f32[128,1,64]{2,1,0:T(1,128)S(1)} all-to-all(f32[128,1,64]{2,1,0:T(1,128)S(1)} %bitcast.22), channel_id=1, replica_groups=mesh['dev'=128] {'dev'}, dimensions={0} | all-to-all | bytes 65536 | tf_op jit(solution)/shard_map/all_to_all | solution.py:250
  38.9 0.0 copy-done.1
  38.9 0.0 copy-done.3
  38.9 1.4 %shard_map.70 = f32[32,256]{1,0:T(8,128)} custom-call(f32[128,64]{1,0:T(8,128)S(1)} %bitcast.18, s32[64,128]{1,0:T(8,128)S(1)} %bitcast.21, f32[32,256]{1,0:T(8,128)S(1)} %bitcast.24, f32[32,256]{1,0:T(8,128)S(1)} %get-tuple-element.9.prob_ref), custom_call_target="tpu_custom_call" | custom-call | tf_op jit(solution)/shard_map/pallas_call | solution.py:239
Async XLA Ops:
  0.6 22.5 %copy-start = (s32[4,1,128,64]{2,3,1,0:T(8,128)S(1)}, s32[4,1,128,64]{2,3,1,0:T(8,128)}, u32[]{:S(2)}) copy-start(s32[4,1,128,64]{2,3,1,0:T(8,128)} %param.9) | copy-start | bytes 393220
  2.2 20.9 %copy-start.2 = (s32[64,128]{1,0:T(8,128)S(1)}, s32[64,128]{1,0:T(8,128)}, u32[]{:S(2)}) copy-start(s32[64,128]{1,0:T(8,128)} %capacity_ref.1) | copy-start | bytes 98308
  24.9 13.9 %copy-start.1 = (s32[1,128,64]{1,2,0:T(8,128)S(1)}, s32[1,128,64]{1,2,0:T(8,128)}, u32[]{:S(2)}) copy-start(s32[1,128,64]{1,2,0:T(8,128)} %param.8) | copy-start | bytes 98308
  25.0 13.9 %copy-start.3 = (f32[256,32]{0,1:T(8,128)S(1)}, f32[256,32]{0,1:T(8,128)}, u32[]{:S(2)}) copy-start(f32[256,32]{0,1:T(8,128)} %param.6) | copy-start | bytes 98308

commit v5 on v4

--- a/solution.py
+++ b/solution.py
@@ -11,9 +11,10 @@
 CELL_DOT = 64
 CELL_BACK = 4
 CELL_BACK_ROWS = 32
-CELL_STACK = 1
 ROUTE_DOT = 64
 SUBLANES = 8
+BY_PRODUCT = 32
+GATHER_DOT = 8
 CELL_ROWS = 64
 ROUTE_ROWS = 64
 PARAMS = pltpu.CompilerParams(vmem_limit_bytes=12 * 1024 * 1024)
@@ -66,6 +67,19 @@
 
 def unfold(x, rows):
     return jnp.concatenate([x[i : i + rows] for i in range(0, x.shape[0], rows)], axis=1)
+
+
+def lane_gather(table_ref, place, lanes):
+    stack = []
+    for t in range(table_ref.shape[0]):
+        entries = jnp.broadcast_to(table_ref[t : t + 1, :], lanes.shape)
+        found = jnp.take_along_axis(entries, lanes, axis=1, mode="promise_in_bounds")
+        depth = 0
+        while stack and stack[-1][1] == depth:
+            found = jnp.where(lax.bitwise_and(place, 1 << depth) != 0, found, stack.pop()[0])
+            depth += 1
+        stack.append((found, depth))
+    return stack[0][0]
 
 
 def gather_kernel(logits_hbm, send_hbm, weight_ref, prob_ref, logits_ref, send_ref, table_ref, held_ref, sems):
@@ -82,22 +96,26 @@
     table_ref[...] = fold(probs, owners)
     routes_in.wait()
     column, row = route_places(send_ref[...], owners)
-    blocks = range(0, slots, SUBLANES)
-    shape = (SUBLANES, owners)
-    columns = [column[i : i + SUBLANES] for i in blocks]
-    rows = [row[i : i + SUBLANES] for i in blocks]
-
-    def take(t, n, found):
-        entries = jnp.broadcast_to(table_ref[t : t + 1, :], shape)
-        entries = jnp.take_along_axis(entries, columns[n], axis=1, mode="promise_in_bounds")
-        return jnp.where(rows[n] == t, entries, found)
-
-    founds = [jnp.zeros(shape, F32) for _ in blocks]
-    for n in range(len(founds)):
-        for t in range(table_ref.shape[0]):
-            founds[n] = take(t, n, founds[n])
-    for n, i in enumerate(blocks):
-        held_ref[i : i + SUBLANES, :] = founds[n]
+    high = table_ref.shape[0]
+    cut = slots - BY_PRODUCT
+    folded = table_ref[...]
+    parts = jnp.concatenate(split(folded), axis=0)
+    column_bf = to_bf(column[cut:])
+    column_places = to_bf(iota(owners, owners))
+    places = iota(high, owners)
+    picked = []
+    for k in range(0, BY_PRODUCT, GATHER_DOT):
+        hots = [marks(hot(column_bf[j : j + 1], column_places)) for j in range(k, k + GATHER_DOT)]
+        found = jnp.dot(parts, jnp.concatenate(hots, axis=1), preferred_element_type=F32)
+        found = found[:high] + found[high:]
+        for j in range(k, k + GATHER_DOT):
+            part = found[:, (j - k) * owners : (j - k + 1) * owners]
+            picked.append(pick(part, row[cut + j : cut + j + 1], places))
+    held_ref[cut:, :] = jnp.concatenate(picked, axis=0)
+    for base in range(0, cut, SUBLANES):
+        lanes, place = column[base : base + SUBLANES], row[base : base + SUBLANES]
+        found = lane_gather(table_ref, place, lanes)
+        held_ref[base : base + SUBLANES, :] = jnp.where(place >= 0, found, 0.0)
     weight_ref[...] = held_ref[...].T
 
 
@@ -136,7 +154,7 @@
     demand_out = pltpu.make_async_copy(demand_ref, demand_hbm, sem)
     demand_out.start()
     pressure = jax.nn.sigmoid(SHARPNESS * (demand - capacity_ref[...].astype(F32)))
-    table = jnp.concatenate(split(pressure), axis=1 - CELL_STACK)
+    table = jnp.concatenate(split(pressure), axis=0)
     places = iota(tiles, sources)
 
     def gather(i, carry):
@@ -145,12 +163,11 @@
         picked = []
         for k in range(0, CELL_BACK_ROWS, CELL_BACK):
             cover = cover_ref[:, pl.ds(pl.multiple_of((base + k) * sources, sources), CELL_BACK * sources)]
-            if CELL_STACK:
-                found = jnp.dot(table, cover, preferred_element_type=F32)
-                found = found[:tiles] + found[tiles:]
-            else:
-                found = jnp.dot(table, jnp.concatenate([cover, cover], axis=0), preferred_element_type=F32)
-            picked += [pick(found[:, (j - k) * sources : (j - k + 1) * sources], tile[j : j + 1], places) for j in range(k, k + CELL_BACK)]
+            found = jnp.dot(table, cover, preferred_element_type=F32)
+            found = found[:tiles] + found[tiles:]
+            for j in range(k, k + CELL_BACK):
+                part = found[:, (j - k) * sources : (j - k + 1) * sources]
+                picked.append(pick(part, tile[j : j + 1], places))
         back_ref[pl.ds(base, CELL_BACK_ROWS), :] = jnp.concatenate(picked, axis=0)
         return carry
 

time: 40.6 us -> 40.4 us (level)
  no operation moved by 1% of the time
where the time goes in v5:
time: 40.4 us; the launch traced here: 40.1 us
  blocking collectives  34.8 us (86%)
  Pallas kernels  4.58 us (11%)
  between operations  0.68 us (2%)
    all_to_all x2, blocking collectives, exchange(): return lax.all_to_all(x, 'dev', split_axis=0, concat_axis=0, tiled=True)  34.8 us
    pallas_call x1, Pallas kernels, cells_call(): pl.pallas_call(cells_kernel, out_shape=(jax.ShapeDtypeStruct((tiles, cell...  1.79 us
    pallas_call x1, Pallas kernels, routes_call(): pl.pallas_call(routes_kernel, out_shape=jax.ShapeDtypeStruct(probs.shape,...  1.4 us
    pallas_call x1, Pallas kernels, gather_call(): pl.pallas_call(gather_kernel, out_shape=(jax.ShapeDtypeStruct((peers, slo...  1.39 us

profile of v5, /device:TPU:1, one launch (start us, length us, event | category | flops | bytes accessed | tf_op | source)
XLA Modules:
  0.0 40.1 jit_solution(9090097816540287793)
XLA Ops:
  0.6 0.0 copy-start
  0.6 1.4 %shard_map.68 = (f32[128,64]{1,0:T(8,128)S(1)}, f32[32,256]{1,0:T(8,128)S(1)}) custom-call(f32[32,256]{1,0:T(8,128)} %bitcast.25, s32[64,128]{1,0:T(8,128)} %bitcast.20), custom_call_target="tpu_custom_call" | custom-call | tf_op jit(solution)/shard_map/pallas_call | solution.py:219
  2.0 0.0 copy-start.2
  2.0 20.9 %all_to_all.22 = f32[128,1,64]{2,1,0:T(1,128)S(1)} all-to-all(f32[128,1,64]{2,1,0:T(1,128)S(1)} %bitcast.23), channel_id=1, replica_groups=mesh['dev'=128] {'dev'}, dimensions={0} | all-to-all | bytes 65536 | tf_op jit(solution)/shard_map/all_to_all | solution.py:267
  23.0 0.0 copy-done
  23.0 0.0 copy-done.2
  23.0 1.8 %shard_map.69 = (f32[64,128]{1,0:T(8,128)}, f32[128,64]{1,0:T(8,128)S(1)}) custom-call(f32[128,64]{1,0:T(8,128)S(1)} %bitcast.17, s32[4,64,128]{2,1,0:T(8,128)S(1)} %bitcast.19, s32[64,128]{1,0:T(8,128)S(1)} %copy-done.2), custom_call_target="tpu_custom_call" | custom-call | tf_op jit(solution)/shard_map/pallas_call | solution.py:239
  24.8 0.0 copy-start.1
  24.8 0.0 copy-start.3
  24.8 13.9 %all_to_all.23 = f32[128,1,64]{2,1,0:T(1,128)S(1)} all-to-all(f32[128,1,64]{2,1,0:T(1,128)S(1)} %bitcast.22), channel_id=1, replica_groups=mesh['dev'=128] {'dev'}, dimensions={0} | all-to-all | bytes 65536 | tf_op jit(solution)/shard_map/all_to_all | solution.py:267
  38.7 0.0 copy-done.1
  38.7 0.0 copy-done.3
  38.7 1.4 %shard_map.70 = f32[32,256]{1,0:T(8,128)} custom-call(f32[128,64]{1,0:T(8,128)S(1)} %bitcast.18, s32[64,128]{1,0:T(8,128)S(1)} %bitcast.21, f32[32,256]{1,0:T(8,128)S(1)} %bitcast.24, f32[32,256]{1,0:T(8,128)S(1)} %get-tuple-element.9.prob_ref), custom_call_target="tpu_custom_call" | custom-call | tf_op jit(solution)/shard_map/pallas_call | solution.py:256
Async XLA Ops:
  0.6 22.3 %copy-start = (s32[4,1,128,64]{2,3,1,0:T(8,128)S(1)}, s32[4,1,128,64]{2,3,1,0:T(8,128)}, u32[]{:S(2)}) copy-start(s32[4,1,128,64]{2,3,1,0:T(8,128)} %param.9) | copy-start | bytes 393220
  2.0 20.9 %copy-start.2 = (s32[64,128]{1,0:T(8,128)S(1)}, s32[64,128]{1,0:T(8,128)}, u32[]{:S(2)}) copy-start(s32[64,128]{1,0:T(8,128)} %capacity_ref.1) | copy-start | bytes 98308
  24.8 13.9 %copy-start.1 = (s32[1,128,64]{1,2,0:T(8,128)S(1)}, s32[1,128,64]{1,2,0:T(8,128)}, u32[]{:S(2)}) copy-start(s32[1,128,64]{1,2,0:T(8,128)} %param.8) | copy-start | bytes 98308
  24.8 13.9 %copy-start.3 = (f32[256,32]{0,1:T(8,128)S(1)}, f32[256,32]{0,1:T(8,128)}, u32[]{:S(2)}) copy-start(f32[256,32]{0,1:T(8,128)} %param.6) | copy-start | bytes 98308

commit v6 on v5

--- a/solution.py
+++ b/solution.py
@@ -10,7 +10,7 @@
 F32 = jnp.float32
 CELL_DOT = 64
 CELL_BACK = 4
-CELL_BACK_ROWS = 32
+CELL_BACK_ROWS = 64
 ROUTE_DOT = 64
 SUBLANES = 8
 BY_PRODUCT = 32
@@ -82,19 +82,24 @@
     return stack[0][0]
 
 
-def gather_kernel(logits_hbm, send_hbm, weight_ref, prob_ref, logits_ref, send_ref, table_ref, held_ref, sems):
+def gather_kernel(
+    logits_hbm, send_hbm, piece_hbm, capacity_hbm, cost_hbm,
+    weight_ref, prob_ref, send_ref, piece_ref, capacity_ref, cost_ref,
+    logits_ref, table_ref, held_ref, sems,
+):
     slots, owners = send_ref.shape
-    scores_in = pltpu.make_async_copy(logits_hbm, logits_ref, sems.at[0])
-    routes_in = pltpu.make_async_copy(send_hbm, send_ref, sems.at[1])
-    scores_in.start()
-    routes_in.start()
-    scores_in.wait()
+    sources = (logits_hbm, send_hbm, piece_hbm.at[pl.ds(1, 3)], capacity_hbm, cost_hbm)
+    places = (logits_ref, send_ref, piece_ref, capacity_ref, cost_ref)
+    copies = [pltpu.make_async_copy(x, y, sems.at[n]) for n, (x, y) in enumerate(zip(sources, places))]
+    for copy in copies:
+        copy.start()
+    copies[0].wait()
     scores = logits_ref[...]
     powers = jnp.exp(scores - jnp.max(scores, axis=0, keepdims=True))
     probs = powers / jnp.sum(powers, axis=0, keepdims=True)
     prob_ref[...] = probs
     table_ref[...] = fold(probs, owners)
-    routes_in.wait()
+    copies[1].wait()
     column, row = route_places(send_ref[...], owners)
     high = table_ref.shape[0]
     cut = slots - BY_PRODUCT
@@ -117,9 +122,11 @@
         found = lane_gather(table_ref, place, lanes)
         held_ref[base : base + SUBLANES, :] = jnp.where(place >= 0, found, 0.0)
     weight_ref[...] = held_ref[...].T
-
-
-def cells_kernel(weight_ref, piece_ref, capacity_ref, demand_hbm, grad_ref, held_ref, back_ref, cover_ref, demand_ref, sem):
+    for copy in copies[2:]:
+        copy.wait()
+
+
+def cells_kernel(weight_ref, piece_ref, capacity_ref, demand_ref, cover_ref, table_ref, held_ref):
     slots, sources = held_ref.shape
     tiles, cells = capacity_ref.shape
     held_ref[...] = weight_ref[...].T
@@ -129,9 +136,9 @@
 
     def add(i, total):
         base = pl.multiple_of(i * CELL_ROWS, CELL_ROWS)
-        tile = to_bf(piece_ref[1, pl.ds(base, CELL_ROWS), :])
-        first = piece_ref[2, pl.ds(base, CELL_ROWS), :]
-        stop = to_bf(first + piece_ref[3, pl.ds(base, CELL_ROWS), :])
+        tile = to_bf(piece_ref[0, pl.ds(base, CELL_ROWS), :])
+        first = piece_ref[1, pl.ds(base, CELL_ROWS), :]
+        stop = to_bf(first + piece_ref[2, pl.ds(base, CELL_ROWS), :])
         first = to_bf(first)
         parts = split(held_ref[pl.ds(base, CELL_ROWS), :])
         for k in range(0, CELL_ROWS, CELL_DOT):
@@ -151,15 +158,21 @@
     total = lax.fori_loop(0, slots // CELL_ROWS, add, jnp.zeros((2 * tiles, cells), F32))
     demand = total[:tiles] + total[tiles:]
     demand_ref[...] = demand
+    pressure = jax.nn.sigmoid(SHARPNESS * (demand - capacity_ref[...].astype(F32)))
+    table_ref[...] = jnp.concatenate(split(pressure), axis=0)
+
+
+def slots_kernel(piece_ref, cover_ref, table_ref, demand_ref, grad_ref, demand_hbm, back_ref, sem):
     demand_out = pltpu.make_async_copy(demand_ref, demand_hbm, sem)
     demand_out.start()
-    pressure = jax.nn.sigmoid(SHARPNESS * (demand - capacity_ref[...].astype(F32)))
-    table = jnp.concatenate(split(pressure), axis=0)
+    slots, sources = back_ref.shape
+    tiles, cells = demand_ref.shape
+    table = table_ref[...]
     places = iota(tiles, sources)
 
     def gather(i, carry):
         base = pl.multiple_of(i * CELL_BACK_ROWS, CELL_BACK_ROWS)
-        tile = piece_ref[1, pl.ds(base, CELL_BACK_ROWS), :]
+        tile = piece_ref[0, pl.ds(base, CELL_BACK_ROWS), :]
         picked = []
         for k in range(0, CELL_BACK_ROWS, CELL_BACK):
             cover = cover_ref[:, pl.ds(pl.multiple_of((base + k) * sources, sources), CELL_BACK * sources)]
@@ -213,43 +226,57 @@
     return [pl.BlockSpec(memory_space=pltpu.HBM)] * count
 
 
-def gather_call(logits, send):
+def gather_call(logits, send, pieces, capacity, route_cost):
     cands, nets = logits.shape
     slots, peers = send.shape
+    arrays = (logits, send, pieces, capacity, route_cost)
     return pl.pallas_call(
         gather_kernel,
-        out_shape=(jax.ShapeDtypeStruct((peers, slots), F32), jax.ShapeDtypeStruct((cands, nets), F32)),
-        in_specs=in_hbm(2),
-        out_specs=tuple(in_vmem(2)),
+        out_shape=(
+            jax.ShapeDtypeStruct((peers, slots), F32),
+            jax.ShapeDtypeStruct((cands, nets), F32),
+            jax.ShapeDtypeStruct(send.shape, send.dtype),
+            jax.ShapeDtypeStruct((3, slots, peers), pieces.dtype),
+            jax.ShapeDtypeStruct(capacity.shape, capacity.dtype),
+            jax.ShapeDtypeStruct((cands, nets), F32),
+        ),
+        in_specs=in_hbm(5),
+        out_specs=tuple(in_vmem(6)),
         compiler_params=PARAMS,
         scratch_shapes=[
             pltpu.VMEM((cands, nets), F32),
-            pltpu.VMEM((slots, peers), jnp.int32),
             pltpu.VMEM((cands * nets // peers, peers), F32),
             pltpu.VMEM((slots, peers), F32),
-            pltpu.SemaphoreType.DMA((2,)),
+            pltpu.SemaphoreType.DMA((5,)),
         ],
-    )(*[pltpu.with_memory_space_constraint(x, pltpu.HBM) for x in (logits, send)])
+    )(*[pltpu.with_memory_space_constraint(x, pltpu.HBM) for x in arrays])
 
 
 def cells_call(weight, pieces, capacity):
     tiles, cells = capacity.shape
     peers, slots = weight.shape
     by_slot = pltpu.VMEM((slots, peers), F32)
-    return pl.pallas_call(
+    demand, cover, table = pl.pallas_call(
         cells_kernel,
-        out_shape=(jax.ShapeDtypeStruct((tiles, cells), F32), jax.ShapeDtypeStruct((peers, slots), F32)),
+        out_shape=(
+            jax.ShapeDtypeStruct((tiles, cells), F32),
+            jax.ShapeDtypeStruct((cells, slots * peers), BF),
+            jax.ShapeDtypeStruct((2 * tiles, cells), BF),
+        ),
         in_specs=in_vmem(3),
-        out_specs=tuple(in_hbm(1) + in_vmem(1)),
+        out_specs=tuple(in_vmem(3)),
         compiler_params=PARAMS,
-        scratch_shapes=[
-            by_slot,
-            by_slot,
-            pltpu.VMEM((cells, slots * peers), BF),
-            pltpu.VMEM((tiles, cells), F32),
-            pltpu.SemaphoreType.DMA,
-        ],
+        scratch_shapes=[by_slot],
     )(weight, pieces, capacity)
+    slot_grad, demand = pl.pallas_call(
+        slots_kernel,
+        out_shape=(jax.ShapeDtypeStruct((peers, slots), F32), jax.ShapeDtypeStruct((tiles, cells), F32)),
+        in_specs=in_vmem(4),
+        out_specs=tuple(in_vmem(1) + in_hbm(1)),
+        compiler_params=PARAMS,
+        scratch_shapes=[by_slot, pltpu.SemaphoreType.DMA],
+    )(pieces, cover, table, demand)
+    return demand, slot_grad
 
 
 def routes_call(slot_grad, send, route_cost, probs):
@@ -268,11 +295,12 @@
 
 
 def body(logits, route_cost, capacity, send_route, recv_piece):
-    send = send_route[0].T
     pieces = jnp.swapaxes(recv_piece[:, 0], 1, 2)
-    weight, probs = gather_call(logits.T, send)
+    weight, probs, send, pieces, capacity, cost = gather_call(
+        logits.T, send_route[0].T, pieces, capacity, route_cost.T
+    )
     demand, slot_grad = cells_call(exchange(weight), pieces, capacity)
-    grad = routes_call(exchange(slot_grad), send, route_cost.T, probs)
+    grad = routes_call(exchange(slot_grad), send, cost, probs)
     return demand, grad.T
 
 

time: 40.4 us -> 40 us (0.990)
    pallas_call x1, Pallas kernels: 1.79 us -> 0.8 us  [cells_call(): pl.pallas_call(cells_kernel, out_shape=(jax.ShapeDtypeStruct((tiles, cell...]
    pallas_call x0 -> x1, Pallas kernels: none -> 0.8 us  [cells_call(): pl.pallas_call(slots_kernel, out_shape=(jax.ShapeDtypeStruct((peers, slot...]
where the time goes in v6:
time: 40 us; the launch traced here: 39.9 us
  blocking collectives  34.8 us (87%)
  Pallas kernels  4.4 us (11%)
  between operations  0.65 us (2%)
    all_to_all x2, blocking collectives, exchange(): return lax.all_to_all(x, 'dev', split_axis=0, concat_axis=0, tiled=True)  34.8 us
    pallas_call x1, Pallas kernels, gather_call(): pl.pallas_call(gather_kernel, out_shape=(jax.ShapeDtypeStruct((peers, slo...  1.4 us
    pallas_call x1, Pallas kernels, routes_call(): pl.pallas_call(routes_kernel, out_shape=jax.ShapeDtypeStruct(probs.shape,...  1.4 us
    pallas_call x1, Pallas kernels, cells_call(): pl.pallas_call(cells_kernel, out_shape=(jax.ShapeDtypeStruct((tiles, cell...  0.8 us
    pallas_call x1, Pallas kernels, cells_call(): pl.pallas_call(slots_kernel, out_shape=(jax.ShapeDtypeStruct((peers, slot...  0.8 us

profile of v6, /device:TPU:1, one launch (start us, length us, event | category | flops | bytes accessed | tf_op | source)
XLA Modules:
  0.0 39.9 jit_solution(12937181613728168687)
XLA Ops:
  0.6 1.4 %shard_map.68 = (f32[128,64]{1,0:T(8,128)S(1)}, f32[32,256]{1,0:T(8,128)S(1)}, s32[64,128]{1,0:T(8,128)S(1)}, s32[3,64,128]{2,1,0:T(8,128)S(1)}, s32[64,128]{1,0:T(8,128)S(1)}, /*index=5*/f32[32,256]{1,0:T(8,128)S(1)}) custom-call(f32[32,256]{1,0:T(8,128)} %bitcast.23, s32[64,128]{1,0:T(8,128)} %bitcast.24, s32[4,64,128]{2,1,0:T(8,128)} %bitcast.21, ...), custom_call_target="tpu_custom_call" | custom-call | tf_op jit(solution)/shard_map/pallas_call | solution.py:233
  2.0 20.9 %all_to_all.22 = f32[128,1,64]{2,1,0:T(1,128)S(1)} all-to-all(f32[128,1,64]{2,1,0:T(1,128)S(1)} %bitcast.19), channel_id=1, replica_groups=mesh['dev'=128] {'dev'}, dimensions={0} | all-to-all | bytes 65536 | tf_op jit(solution)/shard_map/all_to_all | solution.py:294
  22.9 0.8 %shard_map.69 = (f32[64,128]{1,0:T(8,128)S(1)}, bf16[128,8192]{1,0:T(8,128)(2,1)S(1)}, bf16[128,128]{1,0:T(8,128)(2,1)S(1)}) custom-call(f32[128,64]{1,0:T(8,128)S(1)} %bitcast.17, s32[3,64,128]{2,1,0:T(8,128)S(1)} %get-tuple-element.13.piece_ref, s32[64,128]{1,0:T(8,128)S(1)} %get-tuple-element.15.capacity_ref), custom_call_target="tpu_custom_call" | custom-call | tf_op jit(solution)/shard_map/pallas_call | solution.py:259
  23.8 0.8 %shard_map.70 = (f32[128,64]{1,0:T(8,128)S(1)}, f32[64,128]{1,0:T(8,128)}) custom-call(s32[3,64,128]{2,1,0:T(8,128)S(1)} %get-tuple-element.13.piece_ref, bf16[128,8192]{1,0:T(8,128)(2,1)S(1)} %get-tuple-element.16.cover_ref, bf16[128,128]{1,0:T(8,128)(2,1)S(1)} %get-tuple-element.17.table_ref, f32[64,128]{1,0:T(8,128)S(1)} %get-tuple-element.18.demand_ref), custom_call_target="tpu_custom_call" | custom-call | tf_op jit(solution)/shard_map/pallas_call | solution.py:271
  24.6 13.9 %all_to_all.23 = f32[128,1,64]{2,1,0:T(1,128)S(1)} all-to-all(f32[128,1,64]{2,1,0:T(1,128)S(1)} %bitcast.20), channel_id=1, replica_groups=mesh['dev'=128] {'dev'}, dimensions={0} | all-to-all | bytes 65536 | tf_op jit(solution)/shard_map/all_to_all | solution.py:294
  38.5 1.4 %shard_map.71 = f32[32,256]{1,0:T(8,128)} custom-call(f32[128,64]{1,0:T(8,128)S(1)} %bitcast.18, s32[64,128]{1,0:T(8,128)S(1)} %get-tuple-element.21.send_ref, f32[32,256]{1,0:T(8,128)S(1)} %get-tuple-element.22.cost_ref, f32[32,256]{1,0:T(8,128)S(1)} %get-tuple-element.23.prob_ref), custom_call_target="tpu_custom_call" | custom-call | tf_op jit(solution)/shard_map/pallas_call | solution.py:283

commit v7 on v6

--- a/solution.py
+++ b/solution.py
@@ -8,15 +8,9 @@
 SHARPNESS = 2.0
 BF = jnp.bfloat16
 F32 = jnp.float32
-CELL_DOT = 64
-CELL_BACK = 4
-CELL_BACK_ROWS = 64
-ROUTE_DOT = 64
 SUBLANES = 8
 BY_PRODUCT = 32
-GATHER_DOT = 8
-CELL_ROWS = 64
-ROUTE_ROWS = 64
+PRODUCT_ROWS = 4
 PARAMS = pltpu.CompilerParams(vmem_limit_bytes=12 * 1024 * 1024)
 
 
@@ -109,11 +103,11 @@
     column_places = to_bf(iota(owners, owners))
     places = iota(high, owners)
     picked = []
-    for k in range(0, BY_PRODUCT, GATHER_DOT):
-        hots = [marks(hot(column_bf[j : j + 1], column_places)) for j in range(k, k + GATHER_DOT)]
+    for k in range(0, BY_PRODUCT, PRODUCT_ROWS):
+        hots = [marks(hot(column_bf[j : j + 1], column_places)) for j in range(k, k + PRODUCT_ROWS)]
         found = jnp.dot(parts, jnp.concatenate(hots, axis=1), preferred_element_type=F32)
         found = found[:high] + found[high:]
-        for j in range(k, k + GATHER_DOT):
+        for j in range(k, k + PRODUCT_ROWS):
             part = found[:, (j - k) * owners : (j - k + 1) * owners]
             picked.append(pick(part, row[cut + j : cut + j + 1], places))
     held_ref[cut:, :] = jnp.concatenate(picked, axis=0)
@@ -126,94 +120,69 @@
         copy.wait()
 
 
-def cells_kernel(weight_ref, piece_ref, capacity_ref, demand_ref, cover_ref, table_ref, held_ref):
-    slots, sources = held_ref.shape
+def scattered(row, values, high):
+    mask = hot(row, to_bf(iota(high, row.shape[1])))
+    return jnp.concatenate([spread(value, mask) for value in values], axis=0)
+
+
+def cells_kernel(weight_ref, piece_ref, capacity_ref, demand_ref, cover_ref, table_ref):
     tiles, cells = capacity_ref.shape
-    held_ref[...] = weight_ref[...].T
-    tile_places = to_bf(iota(tiles, sources))
-    cell_places = to_bf(iota(cells, sources))
-    width = CELL_ROWS * sources
-
-    def add(i, total):
-        base = pl.multiple_of(i * CELL_ROWS, CELL_ROWS)
-        tile = to_bf(piece_ref[0, pl.ds(base, CELL_ROWS), :])
-        first = piece_ref[1, pl.ds(base, CELL_ROWS), :]
-        stop = to_bf(first + piece_ref[2, pl.ds(base, CELL_ROWS), :])
-        first = to_bf(first)
-        parts = split(held_ref[pl.ds(base, CELL_ROWS), :])
-        for k in range(0, CELL_ROWS, CELL_DOT):
-            lefts, rights = [], []
-            for j in range(k, k + CELL_DOT):
-                mask = hot(tile[j : j + 1], tile_places)
-                lefts.append(jnp.concatenate([spread(part[j : j + 1], mask) for part in parts], axis=0))
-                inside = jnp.logical_and(
-                    cell_places >= jnp.broadcast_to(first[j : j + 1], cell_places.shape),
-                    cell_places < jnp.broadcast_to(stop[j : j + 1], cell_places.shape),
-                )
-                rights.append(marks(inside))
-                cover_ref[:, pl.ds(pl.multiple_of(i * width + j * sources, sources), sources)] = rights[-1]
-            total = total + contract(jnp.concatenate(lefts, axis=1), jnp.concatenate(rights, axis=1))
-        return total
-
-    total = lax.fori_loop(0, slots // CELL_ROWS, add, jnp.zeros((2 * tiles, cells), F32))
+    sources, slots = weight_ref.shape
+    parts = split(weight_ref[...].T)
+    tile = to_bf(piece_ref[0])
+    first = to_bf(piece_ref[1])
+    stop = to_bf(piece_ref[1] + piece_ref[2])
+    places = to_bf(iota(cells, sources))
+    lefts, rights = [], []
+    for j in range(slots):
+        one = slice(j, j + 1)
+        lefts.append(scattered(tile[one], [part[one] for part in parts], tiles))
+        after = places >= jnp.broadcast_to(first[one], places.shape)
+        before = places < jnp.broadcast_to(stop[one], places.shape)
+        rights.append(marks(jnp.logical_and(after, before)))
+        cover_ref[:, j * sources : (j + 1) * sources] = rights[-1]
+    total = contract(jnp.concatenate(lefts, axis=1), jnp.concatenate(rights, axis=1))
     demand = total[:tiles] + total[tiles:]
     demand_ref[...] = demand
     pressure = jax.nn.sigmoid(SHARPNESS * (demand - capacity_ref[...].astype(F32)))
     table_ref[...] = jnp.concatenate(split(pressure), axis=0)
 
 
-def slots_kernel(piece_ref, cover_ref, table_ref, demand_ref, grad_ref, demand_hbm, back_ref, sem):
+def slots_kernel(piece_ref, cover_ref, table_ref, demand_ref, grad_ref, demand_hbm, sem):
     demand_out = pltpu.make_async_copy(demand_ref, demand_hbm, sem)
     demand_out.start()
-    slots, sources = back_ref.shape
-    tiles, cells = demand_ref.shape
-    table = table_ref[...]
+    tiles = demand_ref.shape[0]
+    sources, slots = grad_ref.shape
     places = iota(tiles, sources)
-
-    def gather(i, carry):
-        base = pl.multiple_of(i * CELL_BACK_ROWS, CELL_BACK_ROWS)
-        tile = piece_ref[0, pl.ds(base, CELL_BACK_ROWS), :]
-        picked = []
-        for k in range(0, CELL_BACK_ROWS, CELL_BACK):
-            cover = cover_ref[:, pl.ds(pl.multiple_of((base + k) * sources, sources), CELL_BACK * sources)]
-            found = jnp.dot(table, cover, preferred_element_type=F32)
-            found = found[:tiles] + found[tiles:]
-            for j in range(k, k + CELL_BACK):
-                part = found[:, (j - k) * sources : (j - k + 1) * sources]
-                picked.append(pick(part, tile[j : j + 1], places))
-        back_ref[pl.ds(base, CELL_BACK_ROWS), :] = jnp.concatenate(picked, axis=0)
-        return carry
-
-    lax.fori_loop(0, slots // CELL_BACK_ROWS, gather, 0)
-    grad_ref[...] = back_ref[...].T
+    rows = []
+    for k in range(0, slots, PRODUCT_ROWS):
+        found = jnp.dot(
+            table_ref[...], cover_ref[:, k * sources : (k + PRODUCT_ROWS) * sources], preferred_element_type=F32
+        )
+        found = found[:tiles] + found[tiles:]
+        for j in range(PRODUCT_ROWS):
+            part = found[:, j * sources : (j + 1) * sources]
+            rows.append(pick(part, piece_ref[0, k + j : k + j + 1, :], places))
+    grad_ref[...] = jnp.concatenate(rows, axis=0).T
     demand_out.wait()
 
 
-def routes_kernel(grad_ref, send_ref, cost_ref, prob_ref, out_ref, held_ref):
+def routes_kernel(grad_ref, send_ref, cost_ref, prob_ref, out_ref):
     cands, nets = prob_ref.shape
     slots, owners = send_ref.shape
-    rows = cands * nets // owners
-    held_ref[...] = grad_ref[...].T
-    columns = to_bf(iota(owners, owners))
-    places = to_bf(iota(rows, owners))
-
-    def step(i, total):
-        base = pl.multiple_of(i * ROUTE_ROWS, ROUTE_ROWS)
-        column, row = route_places(send_ref[pl.ds(base, ROUTE_ROWS), :], owners)
-        column, row = to_bf(column), to_bf(row)
-        parts = split(held_ref[pl.ds(base, ROUTE_ROWS), :])
-        for k in range(0, ROUTE_ROWS, ROUTE_DOT):
-            lefts, rights = [], []
-            for j in range(k, k + ROUTE_DOT):
-                mask = hot(row[j : j + 1], places)
-                lefts.append(jnp.concatenate([spread(part[j : j + 1], mask) for part in parts], axis=0))
-                rights.append(marks(hot(column[j : j + 1], columns)))
-            total = total + contract(jnp.concatenate(lefts, axis=1), jnp.concatenate(rights, axis=1))
-        return total
-
-    total = lax.fori_loop(0, slots // ROUTE_ROWS, step, jnp.zeros((2 * rows, owners), F32))
+    high = cands * nets // owners
+    parts = split(grad_ref[...].T)
+    column, row = route_places(send_ref[...], owners)
+    column, row = to_bf(column), to_bf(row)
+    places = to_bf(iota(owners, owners))
+    lefts, rights = [], []
+    for j in range(slots):
+        one = slice(j, j + 1)
+        lefts.append(scattered(row[one], [part[one] for part in parts], high))
+        rights.append(marks(hot(column[one], places)))
+    total = contract(jnp.concatenate(lefts, axis=1), jnp.concatenate(rights, axis=1))
     probs = prob_ref[...]
-    route_grad = cost_ref[...] + unfold(total[:rows] + total[rows:], cands)
+    route_grad = cost_ref[...] + unfold(total[:high] + total[high:], cands)
     expected = jnp.sum(probs * route_grad, axis=0, keepdims=True)
     out_ref[...] = probs * (route_grad - expected)
 
@@ -255,7 +224,6 @@
 def cells_call(weight, pieces, capacity):
     tiles, cells = capacity.shape
     peers, slots = weight.shape
-    by_slot = pltpu.VMEM((slots, peers), F32)
     demand, cover, table = pl.pallas_call(
         cells_kernel,
         out_shape=(
@@ -266,7 +234,6 @@
         in_specs=in_vmem(3),
         out_specs=tuple(in_vmem(3)),
         compiler_params=PARAMS,
-        scratch_shapes=[by_slot],
     )(weight, pieces, capacity)
     slot_grad, demand = pl.pallas_call(
         slots_kernel,
@@ -274,7 +241,7 @@
         in_specs=in_vmem(4),
         out_specs=tuple(in_vmem(1) + in_hbm(1)),
         compiler_params=PARAMS,
-        scratch_shapes=[by_slot, pltpu.SemaphoreType.DMA],
+        scratch_shapes=[pltpu.SemaphoreType.DMA],
     )(pieces, cover, table, demand)
     return demand, slot_grad
 
@@ -286,7 +253,6 @@
         in_specs=in_vmem(4),
         out_specs=pl.BlockSpec(memory_space=pltpu.VMEM),
         compiler_params=PARAMS,
-        scratch_shapes=[pltpu.VMEM(send.shape, F32)],
     )(slot_grad, send, route_cost, probs)
 
 

time: 40 us -> 40 us (level)
  no operation moved by 1% of the time
where the time goes in v7:
time: 40 us; the launch traced here: 39.9 us
  blocking collectives  34.8 us (87%)
  Pallas kernels  4.4 us (11%)
  between operations  0.65 us (2%)
    all_to_all x2, blocking collectives, exchange(): return lax.all_to_all(x, 'dev', split_axis=0, concat_axis=0, tiled=True)  34.8 us
    pallas_call x1, Pallas kernels, routes_call(): pl.pallas_call(routes_kernel, out_shape=jax.ShapeDtypeStruct(probs.shape,...  1.4 us
    pallas_call x1, Pallas kernels, gather_call(): pl.pallas_call(gather_kernel, out_shape=(jax.ShapeDtypeStruct((peers, slo...  1.4 us
    pallas_call x1, Pallas kernels, cells_call(): pl.pallas_call(slots_kernel, out_shape=(jax.ShapeDtypeStruct((peers, slot...  0.8 us

profile of v7, /device:TPU:1, one launch (start us, length us, event | category | flops | bytes accessed | tf_op | source)
XLA Modules:
  0.0 39.9 jit_solution(11756388870663930475)
XLA Ops:
  0.6 1.4 %shard_map.68 = (f32[128,64]{1,0:T(8,128)S(1)}, f32[32,256]{1,0:T(8,128)S(1)}, s32[64,128]{1,0:T(8,128)S(1)}, s32[3,64,128]{2,1,0:T(8,128)S(1)}, s32[64,128]{1,0:T(8,128)S(1)}, /*index=5*/f32[32,256]{1,0:T(8,128)S(1)}) custom-call(f32[32,256]{1,0:T(8,128)} %bitcast.23, s32[64,128]{1,0:T(8,128)} %bitcast.24, s32[4,64,128]{2,1,0:T(8,128)} %bitcast.21, ...), custom_call_target="tpu_custom_call" | custom-call | tf_op jit(solution)/shard_map/pallas_call | solution.py:202
  2.0 20.9 %all_to_all.22 = f32[128,1,64]{2,1,0:T(1,128)S(1)} all-to-all(f32[128,1,64]{2,1,0:T(1,128)S(1)} %bitcast.19), channel_id=1, replica_groups=mesh['dev'=128] {'dev'}, dimensions={0} | all-to-all | bytes 65536 | tf_op jit(solution)/shard_map/all_to_all | solution.py:260
  22.9 0.8 %shard_map.69 = (f32[64,128]{1,0:T(8,128)S(1)}, bf16[128,8192]{1,0:T(8,128)(2,1)S(1)}, bf16[128,128]{1,0:T(8,128)(2,1)S(1)}) custom-call(f32[128,64]{1,0:T(8,128)S(1)} %bitcast.17, s32[3,64,128]{2,1,0:T(8,128)S(1)} %get-tuple-element.13.piece_ref, s32[64,128]{1,0:T(8,128)S(1)} %get-tuple-element.15.capacity_ref), custom_call_target="tpu_custom_call" | custom-call | tf_op jit(solution)/shard_map/pallas_call | solution.py:227
  23.7 0.8 %shard_map.70 = (f32[128,64]{1,0:T(8,128)S(1)}, f32[64,128]{1,0:T(8,128)}) custom-call(s32[3,64,128]{2,1,0:T(8,128)S(1)} %get-tuple-element.13.piece_ref, bf16[128,8192]{1,0:T(8,128)(2,1)S(1)} %get-tuple-element.16.cover_ref, bf16[128,128]{1,0:T(8,128)(2,1)S(1)} %get-tuple-element.17.table_ref, f32[64,128]{1,0:T(8,128)S(1)} %get-tuple-element.18.demand_ref), custom_call_target="tpu_custom_call" | custom-call | tf_op jit(solution)/shard_map/pallas_call | solution.py:238
  24.6 13.9 %all_to_all.23 = f32[128,1,64]{2,1,0:T(1,128)S(1)} all-to-all(f32[128,1,64]{2,1,0:T(1,128)S(1)} %bitcast.20), channel_id=1, replica_groups=mesh['dev'=128] {'dev'}, dimensions={0} | all-to-all | bytes 65536 | tf_op jit(solution)/shard_map/all_to_all | solution.py:260
  38.5 1.4 %shard_map.71 = f32[32,256]{1,0:T(8,128)} custom-call(f32[128,64]{1,0:T(8,128)S(1)} %bitcast.18, s32[64,128]{1,0:T(8,128)S(1)} %get-tuple-element.21.send_ref, f32[32,256]{1,0:T(8,128)S(1)} %get-tuple-element.22.cost_ref, f32[32,256]{1,0:T(8,128)S(1)} %get-tuple-element.23.prob_ref), custom_call_target="tpu_custom_call" | custom-call | tf_op jit(solution)/shard_map/pallas_call | solution.py:250

commit v8 on v7

--- a/solution.py
+++ b/solution.py
@@ -11,6 +11,7 @@
 SUBLANES = 8
 BY_PRODUCT = 32
 PRODUCT_ROWS = 4
+BY_SUMS = 16
 PARAMS = pltpu.CompilerParams(vmem_limit_bytes=12 * 1024 * 1024)
 
 
@@ -148,14 +149,20 @@
     table_ref[...] = jnp.concatenate(split(pressure), axis=0)
 
 
-def slots_kernel(piece_ref, cover_ref, table_ref, demand_ref, grad_ref, demand_hbm, sem):
+def slots_kernel(piece_ref, cover_ref, table_ref, demand_ref, grad_ref, demand_hbm, upto_ref, before_ref, sem):
     demand_out = pltpu.make_async_copy(demand_ref, demand_hbm, sem)
     demand_out.start()
-    tiles = demand_ref.shape[0]
+    tiles, cells = demand_ref.shape
     sources, slots = grad_ref.shape
     places = iota(tiles, sources)
+    cut = slots - BY_SUMS
+    steps = marks(iota(cells, cells) <= lax.broadcasted_iota(jnp.int32, (cells, cells), 1))
+    sums = jnp.dot(table_ref[...], steps, preferred_element_type=F32)
+    upto = sums[:tiles] + sums[tiles:]
+    upto_ref[...] = upto
+    before_ref[...] = upto - (table_ref[:tiles].astype(F32) + table_ref[tiles:].astype(F32))
     rows = []
-    for k in range(0, slots, PRODUCT_ROWS):
+    for k in range(0, cut, PRODUCT_ROWS):
         found = jnp.dot(
             table_ref[...], cover_ref[:, k * sources : (k + PRODUCT_ROWS) * sources], preferred_element_type=F32
         )
@@ -163,6 +170,11 @@
         for j in range(PRODUCT_ROWS):
             part = found[:, j * sources : (j + 1) * sources]
             rows.append(pick(part, piece_ref[0, k + j : k + j + 1, :], places))
+    for k in range(cut, slots, SUBLANES):
+        tile, first, count = (piece_ref[n, k : k + SUBLANES, :] for n in range(3))
+        last = jnp.maximum(first + count - 1, 0)
+        inside = lane_gather(upto_ref, tile, last) - lane_gather(before_ref, tile, first)
+        rows.append(jnp.where(count > 0, inside, 0.0))
     grad_ref[...] = jnp.concatenate(rows, axis=0).T
     demand_out.wait()
 
@@ -241,7 +253,7 @@
         in_specs=in_vmem(4),
         out_specs=tuple(in_vmem(1) + in_hbm(1)),
         compiler_params=PARAMS,
-        scratch_shapes=[pltpu.SemaphoreType.DMA],
+        scratch_shapes=[pltpu.VMEM((tiles, cells), F32), pltpu.VMEM((tiles, cells), F32), pltpu.SemaphoreType.DMA],
     )(pieces, cover, table, demand)
     return demand, slot_grad
 

time: 40 us -> 39.9 us (level)
  no operation moved by 1% of the time
where the time goes in v8:
time: 39.9 us; the launch traced here: 39.8 us
  blocking collectives  34.8 us (87%)
  Pallas kernels  4.29 us (11%)
  between operations  0.65 us (2%)
    all_to_all x2, blocking collectives, exchange(): return lax.all_to_all(x, 'dev', split_axis=0, concat_axis=0, tiled=True)  34.8 us
    pallas_call x1, Pallas kernels, gather_call(): pl.pallas_call(gather_kernel, out_shape=(jax.ShapeDtypeStruct((peers, slo...  1.4 us
    pallas_call x1, Pallas kernels, routes_call(): pl.pallas_call(routes_kernel, out_shape=jax.ShapeDtypeStruct(probs.shape,...  1.4 us
    pallas_call x1, Pallas kernels, cells_call(): pl.pallas_call(cells_kernel, out_shape=(jax.ShapeDtypeStruct((tiles, cell...  0.8 us

profile of v8, /device:TPU:1, one launch (start us, length us, event | category | flops | bytes accessed | tf_op | source)
XLA Modules:
  0.0 39.8 jit_solution(16546822896060378194)
XLA Ops:
  0.6 1.4 %shard_map.68 = (f32[128,64]{1,0:T(8,128)S(1)}, f32[32,256]{1,0:T(8,128)S(1)}, s32[64,128]{1,0:T(8,128)S(1)}, s32[3,64,128]{2,1,0:T(8,128)S(1)}, s32[64,128]{1,0:T(8,128)S(1)}, /*index=5*/f32[32,256]{1,0:T(8,128)S(1)}) custom-call(f32[32,256]{1,0:T(8,128)} %bitcast.23, s32[64,128]{1,0:T(8,128)} %bitcast.24, s32[4,64,128]{2,1,0:T(8,128)} %bitcast.21, ...), custom_call_target="tpu_custom_call" | custom-call | tf_op jit(solution)/shard_map/pallas_call | solution.py:214
  2.0 20.9 %all_to_all.22 = f32[128,1,64]{2,1,0:T(1,128)S(1)} all-to-all(f32[128,1,64]{2,1,0:T(1,128)S(1)} %bitcast.19), channel_id=1, replica_groups=mesh['dev'=128] {'dev'}, dimensions={0} | all-to-all | bytes 65536 | tf_op jit(solution)/shard_map/all_to_all | solution.py:272
  22.9 0.8 %shard_map.69 = (f32[64,128]{1,0:T(8,128)S(1)}, bf16[128,8192]{1,0:T(8,128)(2,1)S(1)}, bf16[128,128]{1,0:T(8,128)(2,1)S(1)}) custom-call(f32[128,64]{1,0:T(8,128)S(1)} %bitcast.17, s32[3,64,128]{2,1,0:T(8,128)S(1)} %get-tuple-element.13.piece_ref, s32[64,128]{1,0:T(8,128)S(1)} %get-tuple-element.15.capacity_ref), custom_call_target="tpu_custom_call" | custom-call | tf_op jit(solution)/shard_map/pallas_call | solution.py:239
  23.7 0.7 %shard_map.70 = (f32[128,64]{1,0:T(8,128)S(1)}, f32[64,128]{1,0:T(8,128)}) custom-call(s32[3,64,128]{2,1,0:T(8,128)S(1)} %get-tuple-element.13.piece_ref, bf16[128,8192]{1,0:T(8,128)(2,1)S(1)} %get-tuple-element.16.cover_ref, bf16[128,128]{1,0:T(8,128)(2,1)S(1)} %get-tuple-element.17.table_ref, f32[64,128]{1,0:T(8,128)S(1)} %get-tuple-element.18.demand_ref), custom_call_target="tpu_custom_call" | custom-call | tf_op jit(solution)/shard_map/pallas_call | solution.py:250
  24.4 13.9 %all_to_all.23 = f32[128,1,64]{2,1,0:T(1,128)S(1)} all-to-all(f32[128,1,64]{2,1,0:T(1,128)S(1)} %bitcast.20), channel_id=1, replica_groups=mesh['dev'=128] {'dev'}, dimensions={0} | all-to-all | bytes 65536 | tf_op jit(solution)/shard_map/all_to_all | solution.py:272
  38.4 1.4 %shard_map.71 = f32[32,256]{1,0:T(8,128)} custom-call(f32[128,64]{1,0:T(8,128)S(1)} %bitcast.18, s32[64,128]{1,0:T(8,128)S(1)} %get-tuple-element.21.send_ref, f32[32,256]{1,0:T(8,128)S(1)} %get-tuple-element.22.cost_ref, f32[32,256]{1,0:T(8,128)S(1)} %get-tuple-element.23.prob_ref), custom_call_target="tpu_custom_call" | custom-call | tf_op jit(solution)/shard_map/pallas_call | solution.py:262

commit v9 on v8

--- a/solution.py
+++ b/solution.py
@@ -80,7 +80,7 @@
 def gather_kernel(
     logits_hbm, send_hbm, piece_hbm, capacity_hbm, cost_hbm,
     weight_ref, prob_ref, send_ref, piece_ref, capacity_ref, cost_ref,
-    logits_ref, table_ref, held_ref, sems,
+    logits_ref, table_ref, sems,
 ):
     slots, owners = send_ref.shape
     sources = (logits_hbm, send_hbm, piece_hbm.at[pl.ds(1, 3)], capacity_hbm, cost_hbm)
@@ -111,12 +111,12 @@
         for j in range(k, k + PRODUCT_ROWS):
             part = found[:, (j - k) * owners : (j - k + 1) * owners]
             picked.append(pick(part, row[cut + j : cut + j + 1], places))
-    held_ref[cut:, :] = jnp.concatenate(picked, axis=0)
+    taken = []
     for base in range(0, cut, SUBLANES):
         lanes, place = column[base : base + SUBLANES], row[base : base + SUBLANES]
         found = lane_gather(table_ref, place, lanes)
-        held_ref[base : base + SUBLANES, :] = jnp.where(place >= 0, found, 0.0)
-    weight_ref[...] = held_ref[...].T
+        taken.append(jnp.where(place >= 0, found, 0.0))
+    weight_ref[...] = jnp.concatenate(taken + picked, axis=0).T
     for copy in copies[2:]:
         copy.wait()
 
@@ -227,7 +227,6 @@
         scratch_shapes=[
             pltpu.VMEM((cands, nets), F32),
             pltpu.VMEM((cands * nets // peers, peers), F32),
-            pltpu.VMEM((slots, peers), F32),
             pltpu.SemaphoreType.DMA((5,)),
         ],
     )(*[pltpu.with_memory_space_constraint(x, pltpu.HBM) for x in arrays])

time: 39.9 us -> 39.9 us (level)
  no operation moved by 1% of the time
where the time goes in v9:
time: 39.9 us; the launch traced here: 39.8 us
  blocking collectives  34.8 us (87%)
  Pallas kernels  4.27 us (11%)
  between operations  0.65 us (2%)
    all_to_all x2, blocking collectives, exchange(): return lax.all_to_all(x, 'dev', split_axis=0, concat_axis=0, tiled=True)  34.8 us
    pallas_call x1, Pallas kernels, routes_call(): pl.pallas_call(routes_kernel, out_shape=jax.ShapeDtypeStruct(probs.shape,...  1.39 us
    pallas_call x1, Pallas kernels, gather_call(): pl.pallas_call(gather_kernel, out_shape=(jax.ShapeDtypeStruct((peers, slo...  1.39 us

profile of v9, /device:TPU:1, one launch (start us, length us, event | category | flops | bytes accessed | tf_op | source)
XLA Modules:
  0.0 39.8 jit_solution(5911179221961993302)
XLA Ops:
  0.6 1.4 %shard_map.68 = (f32[128,64]{1,0:T(8,128)S(1)}, f32[32,256]{1,0:T(8,128)S(1)}, s32[64,128]{1,0:T(8,128)S(1)}, s32[3,64,128]{2,1,0:T(8,128)S(1)}, s32[64,128]{1,0:T(8,128)S(1)}, /*index=5*/f32[32,256]{1,0:T(8,128)S(1)}) custom-call(f32[32,256]{1,0:T(8,128)} %bitcast.23, s32[64,128]{1,0:T(8,128)} %bitcast.24, s32[4,64,128]{2,1,0:T(8,128)} %bitcast.21, ...), custom_call_target="tpu_custom_call" | custom-call | tf_op jit(solution)/shard_map/pallas_call | solution.py:214
  2.0 20.9 %all_to_all.22 = f32[128,1,64]{2,1,0:T(1,128)S(1)} all-to-all(f32[128,1,64]{2,1,0:T(1,128)S(1)} %bitcast.19), channel_id=1, replica_groups=mesh['dev'=128] {'dev'}, dimensions={0} | all-to-all | bytes 65536 | tf_op jit(solution)/shard_map/all_to_all | solution.py:271
  22.9 0.8 %shard_map.69 = (f32[64,128]{1,0:T(8,128)S(1)}, bf16[128,8192]{1,0:T(8,128)(2,1)S(1)}, bf16[128,128]{1,0:T(8,128)(2,1)S(1)}) custom-call(f32[128,64]{1,0:T(8,128)S(1)} %bitcast.17, s32[3,64,128]{2,1,0:T(8,128)S(1)} %get-tuple-element.13.piece_ref, s32[64,128]{1,0:T(8,128)S(1)} %get-tuple-element.15.capacity_ref), custom_call_target="tpu_custom_call" | custom-call | tf_op jit(solution)/shard_map/pallas_call | solution.py:238
  23.7 0.7 %shard_map.70 = (f32[128,64]{1,0:T(8,128)S(1)}, f32[64,128]{1,0:T(8,128)}) custom-call(s32[3,64,128]{2,1,0:T(8,128)S(1)} %get-tuple-element.13.piece_ref, bf16[128,8192]{1,0:T(8,128)(2,1)S(1)} %get-tuple-element.16.cover_ref, bf16[128,128]{1,0:T(8,128)(2,1)S(1)} %get-tuple-element.17.table_ref, f32[64,128]{1,0:T(8,128)S(1)} %get-tuple-element.18.demand_ref), custom_call_target="tpu_custom_call" | custom-call | tf_op jit(solution)/shard_map/pallas_call | solution.py:249
  24.4 13.9 %all_to_all.23 = f32[128,1,64]{2,1,0:T(1,128)S(1)} all-to-all(f32[128,1,64]{2,1,0:T(1,128)S(1)} %bitcast.20), channel_id=1, replica_groups=mesh['dev'=128] {'dev'}, dimensions={0} | all-to-all | bytes 65536 | tf_op jit(solution)/shard_map/all_to_all | solution.py:271
  38.4 1.4 %shard_map.71 = f32[32,256]{1,0:T(8,128)} custom-call(f32[128,64]{1,0:T(8,128)S(1)} %bitcast.18, s32[64,128]{1,0:T(8,128)S(1)} %get-tuple-element.21.send_ref, f32[32,256]{1,0:T(8,128)S(1)} %get-tuple-element.22.cost_ref, f32[32,256]{1,0:T(8,128)S(1)} %get-tuple-element.23.prob_ref), custom_call_target="tpu_custom_call" | custom-call | tf_op jit(solution)/shard_map/pallas_call | solution.py:261
